TPU v7x, 32 devices: a whole 2x2x4 slice. The times are simulated.
32 devices in a mesh: groups: 2 (over x), feat: 8 (over z, y), tgt: 2 (over core).
Axes of the slice: x: 2, y: 2, z: 4, core: 2. Of those that a mesh axis runs over, the one named last changes fastest.
Arguments:
- inputs: float32 [1536, 2304], P(('groups', 'feat')), parts along dimension 0, may hold values from -6 to 6
- preacts: bfloat16 [1536, 16384], P('groups', 'feat'), parts along dimension 0, may hold values from -6 to 6
- cotangent: float32 [2, 1536, 2304], P('tgt', ('groups', 'feat')), parts along dimension 1, may hold values from -1.5 to 1.5
- w_enc: bfloat16 [2304, 16384], P(None, 'feat'), may hold values from -0.125 to 0.125
- w_dec: bfloat16 [2, 16384, 2304], P('tgt', 'feat'), may hold values from -0.046875 to 0.046875
Outputs:
- grad_dec: float32 [4, 16384, 2304], P(('groups', 'tgt'), 'feat'), parts along dimension 0
- grad_enc: float32 [4608, 16384], P(('groups', 'tgt'), 'feat'), parts along dimension 0
- grad_bias: float32 [32768], P(('groups', 'feat')), parts along dimension 0
- grad_inputs: float32 [1536, 2304], P(('groups', 'feat'), 'tgt'), parts along dimension 0
There are 2 independent parts, one for each index of `groups`. A program takes and returns all parts, laid end to end along the dimension named above; an argument that names none is the same for every part. Nothing has to cross between parts.
All inputs are finite; a program needn't handle non-finite values.
Results may differ from a plain program's by a relative error of at most 0.005.
Values may be sent and summed in bfloat16 or wider, within the bound.
A program may use at most 128 MiB of HBM per device.

v0:
```python
import jax
import jax.numpy as jnp
from jax import lax
from jax.sharding import PartitionSpec as P


def body(inputs, preacts, cotangent, w_enc, w_dec):
    active = jnp.maximum(preacts, 0)
    back_rows = cotangent.astype(jnp.bfloat16)
    back_all = lax.all_gather(back_rows, "feat", axis=1, tiled=True)
    grad_dec = jnp.einsum("tf,ltd->lfd", active, back_all, preferred_element_type=jnp.float32)
    partial_value = jnp.einsum("ltd,lfd->tf", back_all, w_dec, preferred_element_type=jnp.float32)
    tgt_index = lax.axis_index("tgt")
    summed = lax.psum(partial_value, "tgt")
    pre_grad = jnp.where(preacts > 0, summed, jnp.zeros_like(summed)).astype(jnp.bfloat16)
    grad_bias = jnp.sum(pre_grad.astype(jnp.float32), axis=0)
    half_width = inputs.shape[1] // lax.axis_size("tgt")
    input_half = lax.dynamic_slice_in_dim(inputs, tgt_index * half_width, half_width, 1).astype(
        jnp.bfloat16
    )
    input_all = lax.all_gather(input_half, "feat", axis=0, tiled=True)
    grad_enc = lax.dot_general(
        input_all, pre_grad, (((0,), (0,)), ((), ())), preferred_element_type=jnp.float32
    )
    enc_half = lax.dynamic_slice_in_dim(w_enc, tgt_index * half_width, half_width, 0)
    grad_inputs = lax.psum_scatter(
        lax.dot_general(
            pre_grad, enc_half, (((1,), (1,)), ((), ())), preferred_element_type=jnp.float32
        ),
        "feat",
        scatter_dimension=0,
        tiled=True,
    )
    return (grad_dec, grad_enc, grad_bias, grad_inputs)


def solution(mesh):
    in_specs = (
        P(("groups", "feat"), None),
        P("groups", "feat"),
        P("tgt", ("groups", "feat"), None),
        P(None, "feat"),
        P("tgt", "feat", None),
    )
    out_specs = (
        P(("groups", "tgt"), "feat", None),
        P(("groups", "tgt"), "feat"),
        P(("groups", "feat")),
        P(("groups", "feat"), "tgt"),
    )
    return jax.shard_map(body, mesh=mesh, in_specs=in_specs, out_specs=out_specs, check_vma=False)
```

profile of v0, /device:TPU:0, one launch (start us, length us, event | category | flops | bytes accessed | tf_op | source)
XLA Modules:
  0.0 214.8 jit_solution(9843762855470971217)
XLA Ops:
  7.2 0.0 copy-start
  7.2 0.0 all-gather.3.cloned.1.call-start
  7.2 2.0 convert_element_type.12
  9.3 0.0 all-gather.3.cloned.1.call-update
  9.3 0.0 all-gather.5.cloned.1.call-start
  9.4 0.0 copy-done
  9.4 0.7 dynamic-slice_convert_fusion
  10.1 0.0 all-gather.5.cloned.1.call-update
  10.1 0.0 reduce-scatter.2.cloned.1.call-start
  10.2 68.5 %all-gather.3.cloned.1.call-done = bf16[1,768,2304]{2,1,0:T(8,128)(2,1)} async-done(((bf16[1,96,2304]{2,1,0:T(8,128)(2,1)}), bf16[1,768,2304]{2,1,0:T(8,128)(2,1)}) %all-gather.3.cloned.1.call-update) | async-done | bytes 3538960 | tf_op jit(solution)/shard_map/all_gather | solution.py:10
  78.7 12.8 %fusion = f32[768,2048]{1,0:T(8,128)} fusion(bf16[1,2048,2304]{2,1,0:T(8,128)(2,1)} %param.9, bf16[1,768,2304]{2,1,0:T(8,128)(2,1)} %all-gather.3.cloned.1.call-done), kind=kOutput, calls=%fused_computation.1 | convolution fusion | flops 7247757312 | bytes 19267584 | tf_op jit(solution)/shard_map/ltd,lfd->tf/dot_general | solution.py:12
  91.5 20.5 %all-reduce.1 = bf16[768,2048]{1,0:T(8,128)(2,1)S(1)} all-reduce(f32[768,2048]{1,0:T(8,128)} %fusion), channel_id=1, replica_groups=mesh['groups'=2,'feat'=8,'tgt'=2] {'tgt'}, use_global_device_ids=true, to_apply=%region_0.0 | all-reduce | flops 1572864 | bytes 9437184 | tf_op jit(solution)/shard_map/psum | solution.py:14
  111.9 3.7 %convert_reduce_fusion = (f32[2048]{0:T(1024)}, bf16[768,2048]{1,0:T(8,128)(2,1)S(1)}) fusion(bf16[768,2048]{1,0:T(8,128)(2,1)S(1)} %all-reduce.1, bf16[768,2048]{1,0:T(8,128)(2,1)} %param.6), kind=kLoop, calls=%fused_computation.3 | loop fusion | flops 9435136 | bytes 9445376 | tf_op jit(solution)/shard_map/reduce_sum | solution.py:16
  115.6 0.0 copy-start.3
  115.6 1.7 copy-done.3
  117.3 8.4 %fusion.2 = f32[768,1152]{1,0:T(8,128)} fusion(bf16[768,2048]{1,0:T(8,128)(2,1)S(1)} %get-tuple-element.5, bf16[2304,2048]{1,0:T(8,128)(2,1)} %param.8, s32[]{:T(128)S(6)} %select_n.8), kind=kOutput, calls=%fused_computation.5 | convolution fusion | flops 3623878656 | bytes 11403268 | tf_op jit(solution)/shard_map/dot_general | solution.py:27
  125.7 0.0 copy-start.4
  125.7 0.0 reduce-scatter.2.cloned.1.call-update
  125.8 0.2 all-gather.5.cloned.1.call-done
  125.9 1.7 copy-done.4
  127.6 0.0 copy-start.2
  127.6 0.0 copy-start.5
  127.6 7.9 %fusion.10 = f32[1152,2048]{1,0:T(8,128)} fusion(bf16[768,1152]{1,0:T(8,128)(2,1)} %all-gather.5.cloned.1.call-done, bf16[768,2048]{1,0:T(8,128)(2,1)S(1)} %copy-done.4), kind=kOutput, calls=%fused_computation.14 | convolution fusion | flops 3623878656 | bytes 14352384 | tf_op jit(solution)/shard_map/dot_general | solution.py:22
  135.5 0.0 copy-done.2
  135.5 0.0 copy-done.5
  135.5 0.0 copy-start.1
  135.5 10.9 %convolution_bitcast_fusion = f32[1,2048,2304]{2,1,0:T(8,128)} fusion(bf16[1,768,2304]{2,1,0:T(8,128)(2,1)S(1)} %copy-done.5, bf16[768,2048]{1,0:T(8,128)(2,1)S(1)} %copy-done.2), kind=kOutput, calls=%fused_computation | convolution fusion | flops 7249330176 | bytes 25559040 | tf_op jit(solution)/shard_map/tf,ltd->lfd/dot_general | solution.py:11
  146.4 61.9 %reduce-scatter.2.cloned.1.call-done = f32[96,1152]{1,0:T(8,128)} async-done(((f32[768,1152]{1,0:T(8,128)}), f32[96,1152]{1,0:T(8,128)}) %reduce-scatter.2.cloned.1.call-update) | async-done | bytes 442384 | tf_op jit(solution)/shard_map/reduce_scatter | solution.py:26
  208.3 0.0 copy-done.1
Async XLA Ops:
  7.2 2.2 %copy-start = (f32[96,2304]{1,0:T(8,128)S(1)}, f32[96,2304]{1,0:T(8,128)}, u32[]{:S(2)}) copy-start(f32[96,2304]{1,0:T(8,128)} %param.5) | copy-start | bytes 2654212
  7.2 71.5 %all-gather.3.cloned.1.call-start = ((), (), s32[]{:S(2)}) async-start(), calls=%async_computation.1 | async-start | bytes 3981312 | tf_op jit(solution)/shard_map/all_gather | solution.py:10
  9.3 116.6 %all-gather.5.cloned.1.call-start = ((), (), s32[]{:S(2)}) async-start(), calls=%async_computation.2 | async-start | bytes 1990656 | tf_op jit(solution)/shard_map/all_gather | solution.py:21
  10.1 198.2 %reduce-scatter.2.cloned.1.call-start = ((), (), s32[]{:S(2)}) async-start(), calls=%async_computation.3 | async-start | bytes 3981312 | tf_op jit(solution)/shard_map/reduce_scatter | solution.py:26
  115.6 1.7 copy-start.3
  125.7 1.9 copy-start.4
  127.6 7.9 %copy-start.2 = (bf16[768,2048]{1,0:T(8,128)(2,1)S(1)}, bf16[768,2048]{1,0:T(8,128)(2,1)}, u32[]{:S(2)}) copy-start(bf16[768,2048]{1,0:T(8,128)(2,1)} %param.6) | copy-start | bytes 9437188
  127.6 7.9 %copy-start.5 = (bf16[1,768,2304]{2,1,0:T(8,128)(2,1)S(1)}, bf16[1,768,2304]{2,1,0:T(8,128)(2,1)}, u32[]{:S(2)}) copy-start(bf16[1,768,2304]{2,1,0:T(8,128)(2,1)} %all-gather.3.cloned.1.call-done) | copy-start | bytes 10616836
  135.5 72.8 %copy-start.1 = (f32[96,2304]{1,0:T(8,128)S(1)}, f32[96,2304]{1,0:T(8,128)}, u32[]{:S(2)}) copy-start(f32[96,2304]{1,0:T(8,128)} %param.5) | copy-start | bytes 2654212
Sparse Core Ops, SparseCore 0:
  10.8 67.8 all-gather.2
  81.4 44.4 all-gather.4
  130.1 78.1 reduce-scatter.1
where the time goes:
time: 215 us
  waiting for transfers between devices  131 us (61%)
  matrix products  40 us (19%)
  blocking collectives  20.5 us (10%)
  between operations  13.8 us (6%)
  other arithmetic  5.73 us (3%)
  local copies, waits for them, and re-layouts  4.11 us (2%)
    all_gather x1, waiting for transfers between devices, body(): back_all = lax.all_gather(back_rows, 'feat', axis=1, tiled=True)  68.5 us
    reduce_scatter x1, waiting for transfers between devices, body(): lax.psum_scatter(lax.dot_general(pre_grad, enc_half, (((1,), (1,)), ((),...  61.9 us
    psum x1, blocking collectives, body(): summed = lax.psum(partial_value, 'tgt')  20.5 us
    dot_general x1, matrix products, body(): jnp.einsum('ltd,lfd->tf', back_all, w_dec, preferred_element_type=jnp.flo...  12.8 us
    dot_general x1, matrix products, body(): jnp.einsum('tf,ltd->lfd', active, back_all, preferred_element_type=jnp.fl...  10.9 us
    dot_general x1, matrix products, body(): lax.dot_general(pre_grad, enc_half, (((1,), (1,)), ((), ())), preferred_e...  8.43 us
    dot_general x1, matrix products, body(): lax.dot_general(input_all, pre_grad, (((0,), (0,)), ((), ())), preferred_...  7.88 us
  transfers between devices with their start and end apart: 3, of which 3 were waited for; matrix products, arithmetic and copies ran while one was open for 21% of the time, Pallas kernels for 0%

commit v1 on v0

v1 whole, which is shorter than its diff:
```python
import functools

import jax
import jax.numpy as jnp
from jax import lax
from jax.experimental import pallas as pl
from jax.experimental.pallas import tpu as pltpu
from jax.sharding import PartitionSpec as P

MESH = pl.DeviceIdType.MESH


def gather_kernel(n, cot_ref, all_ref, up_sem, down_sem, side_sem, recv_sem):
    deep = n // 2
    me = lax.axis_index("feat")
    z, y = me // 2, lax.rem(me, 2)
    mate = 2 * z + 1 - y

    def to(block, sem, target):
        return pltpu.make_async_remote_copy(
            src_ref=all_ref.at[block],
            dst_ref=all_ref.at[block],
            send_sem=sem,
            recv_sem=recv_sem.at[block],
            device_id={"feat": target},
            device_id_type=MESH,
        )

    all_ref[me] = cot_ref[...].astype(jnp.bfloat16)

    barrier = pltpu.get_barrier_semaphore()
    pl.semaphore_signal(barrier, inc=1, device_id={"feat": mate}, device_id_type=MESH)

    @pl.when(z + 1 < deep)
    def _():
        pl.semaphore_signal(barrier, inc=1, device_id={"feat": me + 2}, device_id_type=MESH)

    @pl.when(z > 0)
    def _():
        pl.semaphore_signal(barrier, inc=1, device_id={"feat": me - 2}, device_id_type=MESH)

    pl.semaphore_wait(barrier, 1 + jnp.where(z + 1 < deep, 1, 0) + jnp.where(z > 0, 1, 0))

    to(me, side_sem.at[z], mate).start()

    @pl.when(z + 1 < deep)
    def _():
        to(me, up_sem.at[z], me + 2).start()

    @pl.when(z > 0)
    def _():
        to(me, down_sem.at[z], me - 2).start()

    for step in range(1, deep):
        low, high = z - step, z + step

        @pl.when(low >= 0)
        def _():
            block = 2 * low + y
            to(block, side_sem.at[low], mate).wait_recv()

            @pl.when(z + 1 < deep)
            def _():
                to(block, up_sem.at[low], me + 2).start()

            to(block, side_sem.at[low], mate).start()

        @pl.when(high < deep)
        def _():
            block = 2 * high + y
            to(block, side_sem.at[high], mate).wait_recv()

            @pl.when(z > 0)
            def _():
                to(block, down_sem.at[high], me - 2).start()

            to(block, side_sem.at[high], mate).start()

    for row in range(deep):
        to(2 * row + 1 - y, side_sem.at[row], mate).wait_recv()
    for row in range(deep):
        block = 2 * row + y
        to(block, side_sem.at[row], mate).wait_send()

        @pl.when((row <= z) & (z + 1 < deep))
        def _():
            to(block, up_sem.at[row], mate).wait_send()

        @pl.when((row >= z) & (z > 0))
        def _():
            to(block, down_sem.at[row], mate).wait_send()


def gather(cot, n):
    tok, width = cot.shape
    deep = n // 2
    return pl.pallas_call(
        functools.partial(gather_kernel, n),
        out_shape=jax.ShapeDtypeStruct((n, tok, width), jnp.bfloat16),
        in_specs=[pl.BlockSpec(memory_space=pltpu.VMEM)],
        out_specs=pl.BlockSpec(memory_space=pltpu.VMEM),
        scratch_shapes=[
            pltpu.SemaphoreType.DMA((deep,)),
            pltpu.SemaphoreType.DMA((deep,)),
            pltpu.SemaphoreType.DMA((deep,)),
            pltpu.SemaphoreType.DMA((n,)),
        ],
        compiler_params=pltpu.CompilerParams(
            collective_id=0, has_side_effects=True, vmem_limit_bytes=24 * 1024 * 1024
        ),
        cost_estimate=pl.CostEstimate(
            flops=0, bytes_accessed=40 * n * tok * width, transcendentals=0
        ),
    )(cot)


def body(inputs, preacts, cotangent, w_enc, w_dec):
    n = lax.axis_size("feat")
    deep = n // 2
    tok = inputs.shape[0]
    f_loc = preacts.shape[1]
    me = lax.axis_index("feat")
    z, y = me // 2, lax.rem(me, 2)
    tgt_index = lax.axis_index("tgt")
    half_width = inputs.shape[1] // lax.axis_size("tgt")

    back_all = gather(cotangent[0], n)
    input_half = lax.dynamic_slice_in_dim(inputs, tgt_index * half_width, half_width, 1).astype(
        jnp.bfloat16
    )
    back_all, input_half = lax.optimization_barrier((back_all, input_half))
    input_all = lax.all_gather(input_half, "feat", axis=0, tiled=True)
    back_all = back_all.reshape(n * tok, -1)

    partial_value = lax.dot_general(
        back_all, w_dec[0], (((1,), (1,)), ((), ())), preferred_element_type=jnp.float32
    ).astype(jnp.bfloat16)
    other = lax.ppermute(partial_value, "tgt", [(0, 1), (1, 0)])
    summed = partial_value.astype(jnp.float32) + other.astype(jnp.float32)
    pre_grad = jnp.where(preacts > 0, summed, jnp.zeros_like(summed)).astype(jnp.bfloat16)
    grad_bias = jnp.sum(pre_grad.astype(jnp.float32), axis=0)

    enc_half = lax.dynamic_slice_in_dim(w_enc, tgt_index * half_width, half_width, 0)
    part = lax.dot_general(
        pre_grad, enc_half, (((1,), (1,)), ((), ())), preferred_element_type=jnp.float32
    ).astype(jnp.bfloat16)
    part = part.reshape(deep, 2, tok, half_width)
    theirs = lax.dynamic_index_in_dim(part, 1 - y, 1, keepdims=False)
    mine = lax.dynamic_index_in_dim(part, y, 1, keepdims=False)
    arrived = lax.ppermute(theirs, "feat", [(i, i ^ 1) for i in range(n)])

    active = jnp.maximum(preacts, 0)
    grad_dec = lax.dot_general(
        active, back_all, (((0,), (0,)), ((), ())), preferred_element_type=jnp.float32
    )[None]

    both = mine.astype(jnp.float32) + arrived.astype(jnp.float32)
    total = lax.dynamic_index_in_dim(both, z, 0, keepdims=False)
    sent = both.astype(jnp.bfloat16)
    for step in range(1, deep):
        block = lax.dynamic_index_in_dim(sent, lax.rem(z + step, deep), 0, keepdims=False)
        got = lax.ppermute(block, "feat", [(i, (i + 2 * step) % n) for i in range(n)])
        total = total + got.astype(jnp.float32)
    grad_enc = lax.dot_general(
        input_all, pre_grad, (((0,), (0,)), ((), ())), preferred_element_type=jnp.float32
    )
    return (grad_dec, grad_enc, grad_bias, total)


def solution(mesh):
    in_specs = (
        P(("groups", "feat"), None),
        P("groups", "feat"),
        P("tgt", ("groups", "feat"), None),
        P(None, "feat"),
        P("tgt", "feat", None),
    )
    out_specs = (
        P(("groups", "tgt"), "feat", None),
        P(("groups", "tgt"), "feat"),
        P(("groups", "feat")),
        P(("groups", "feat"), "tgt"),
    )
    return jax.shard_map(body, mesh=mesh, in_specs=in_specs, out_specs=out_specs, check_vma=False)
```

time: 215 us -> 151 us (0.70)
  waiting for transfers between devices: 131 us -> 33.9 us
  Pallas kernels: 0 us -> 45.3 us
  blocking collectives: 20.5 us -> 0 us
  starting transfers between devices: 0.12 us -> 4.61 us
  other arithmetic: 5.73 us -> 9.83 us
  matrix products: 40 us -> 37.5 us
    all_gather x1 -> x0, waiting for transfers between devices: 68.5 us -> none  [body(): back_all = lax.all_gather(back_rows, 'feat', axis=1, tiled=True)]
    reduce_scatter x1 -> x0, waiting for transfers between devices: 61.9 us -> none  [body(): lax.psum_scatter(lax.dot_general(pre_grad, enc_half, (((1,), (1,)), ((),...]
    pallas_call x0 -> x1, Pallas kernels: none -> 45.3 us  [gather(): pl.pallas_call(functools.partial(gather_kernel, n), out_shape=jax.ShapeDt...]
    ppermute x0 -> x5, waiting for transfers between devices: none -> 33.9 us  [the longest x1 19.7 us: body(): arrived = lax.ppermute(theirs, 'feat', [(i, i ^ 1) for i in range(n)])]
    psum x1 -> x0, blocking collectives: 20.5 us -> none  [body(): summed = lax.psum(partial_value, 'tgt')]
    ppermute x0 -> x5, starting transfers between devices: none -> 4.57 us  [the longest x3 3.83 us: body(): lax.ppermute(block, 'feat', [(i, (i + 2 * step) % n) for i in range(n)])]
    dot_general x1, matrix products: 8.43 us -> 4.28 us  [body(): lax.dot_general(pre_grad, enc_half, (((1,), (1,)), ((), ())), preferred_e...]
    reduce_sum x1, other arithmetic: 3.68 us -> 6.66 us  [body(): grad_bias = jnp.sum(pre_grad.astype(jnp.float32), axis=0)]
  transfers between devices with their start and end apart: 3 -> 6, of which waited for: 3 -> 3; matrix products, arithmetic and copies ran while one was open for 21% -> 23% of each run, Pallas kernels for 0% -> 0%
where the time goes in v1:
time: 151 us
  Pallas kernels  45.3 us (30%)
  matrix products  37.5 us (25%)
  waiting for transfers between devices  33.9 us (22%)
  between operations  14.1 us (9%)
  other arithmetic  9.83 us (7%)
  local copies, waits for them, and re-layouts  5.85 us (4%)
  starting transfers between devices  4.61 us (3%)
    pallas_call x1, Pallas kernels, gather(): pl.pallas_call(functools.partial(gather_kernel, n), out_shape=jax.ShapeDt...  45.3 us
    ppermute x1, waiting for transfers between devices, body(): arrived = lax.ppermute(theirs, 'feat', [(i, i ^ 1) for i in range(n)])  19.7 us
    dot_general x1, matrix products, body(): lax.dot_general(back_all, w_dec[0], (((1,), (1,)), ((), ())), preferred_e...  12.3 us
    dot_general x1, matrix products, body(): lax.dot_general(active, back_all, (((0,), (0,)), ((), ())), preferred_ele...  10.8 us
    dot_general x1, matrix products, body(): lax.dot_general(input_all, pre_grad, (((0,), (0,)), ((), ())), preferred_...  10.1 us
    ppermute x3, waiting for transfers between devices, body(): lax.ppermute(block, 'feat', [(i, (i + 2 * step) % n) for i in range(n)])  8.27 us
    reduce_sum x1, other arithmetic, body(): grad_bias = jnp.sum(pre_grad.astype(jnp.float32), axis=0)  6.66 us
    ppermute x1, waiting for transfers between devices, body(): other = lax.ppermute(partial_value, 'tgt', [(0, 1), (1, 0)])  5.96 us
  transfers between devices with their start and end apart: 6, of which 3 were waited for; matrix products, arithmetic and copies ran while one was open for 23% of the time, Pallas kernels for 0%

profile of v1, /device:TPU:0, one launch (start us, length us, event | category | flops | bytes accessed | tf_op | source)
XLA Modules:
  0.0 151.1 jit_solution(10811710925659347312)
XLA Ops:
  7.2 0.0 copy-start
  7.2 0.0 all-gather.2.cloned.1.call-start
  7.2 0.0 copy-start.4
  7.2 1.2 copy-done.4
  8.5 45.3 %shard_map.84 = bf16[8,96,2304]{2,1,0:T(8,128)(2,1)S(1)} custom-call(f32[96,2304]{1,0:T(8,128)S(1)} %bitcast.35), custom_call_target="tpu_custom_call" | custom-call | bytes 70778880 | tf_op jit(solution)/shard_map/pallas_call | solution.py:97
  53.7 0.0 copy-start.2
  53.8 1.8 %copy-done.2 = bf16[8,96,2304]{2,1,0:T(8,128)(2,1)} copy-done((bf16[8,96,2304]{2,1,0:T(8,128)(2,1)}, bf16[8,96,2304]{2,1,0:T(8,128)(2,1)S(1)}, u32[]{:S(2)}) %copy-start.2) | copy-done | bytes 3538968
  55.5 0.0 copy-done
  55.5 0.7 dynamic-slice_convert_fusion
  56.3 12.3 %fusion.7 = bf16[768,2048]{1,0:T(8,128)(2,1)} fusion(bf16[768,2304]{1,0:T(8,128)(2,1)} %bitcast.33, bf16[1,2048,2304]{2,1,0:T(8,128)(2,1)} %param.9), kind=kOutput, calls=%fused_computation.8 | convolution fusion | flops 7249330176 | bytes 16121856 | tf_op jit(solution)/shard_map/dot_general | solution.py:135
  68.5 0.0 collective-permute-start
  68.5 0.0 all-gather.2.cloned.1.call-update
  68.6 0.0 copy-start.8
  68.6 6.0 %collective-permute-done = bf16[768,2048]{1,0:T(8,128)(2,1)} collective-permute-done((bf16[768,2048]{1,0:T(8,128)(2,1)}, bf16[768,2048]{1,0:T(8,128)(2,1)}, u32[]{:S(2)}, u32[]{:S(2)}) %collective-permute-start) | collective-permute-done | bytes 3145760 | tf_op jit(solution)/shard_map/ppermute | solution.py:138
  74.5 6.7 %convert_reduce_fusion = (f32[2048]{0:T(1024)}, bf16[768,2048]{1,0:T(8,128)(2,1)S(1)}) fusion(bf16[768,2048]{1,0:T(8,128)(2,1)} %collective-permute-done, bf16[768,2048]{1,0:T(8,128)(2,1)} %fusion.7, bf16[768,2048]{1,0:T(8,128)(2,1)} %param.6), kind=kLoop, calls=%fused_computation.3 | loop fusion | flops 12580864 | bytes 12591104 | tf_op jit(solution)/shard_map/reduce_sum | solution.py:141
  81.2 0.0 copy-done.8
  81.2 4.3 %fusion.4 = bf16[768,1152]{1,0:T(8,128)(2,1)S(1)} fusion(bf16[768,2048]{1,0:T(8,128)(2,1)S(1)} %get-tuple-element.11, bf16[2304,2048]{1,0:T(8,128)(2,1)S(1)} %copy-done.8, s32[]{:T(128)S(6)} %select_n.34), kind=kOutput, calls=%fused_computation.7 | convolution fusion | flops 3624763392 | bytes 9633796 | tf_op jit(solution)/shard_map/dot_general | solution.py:144
  85.5 1.3 copy-done.7
  86.8 0.1 dynamic-slice_bitcast_fusion
  86.9 0.7 collective-permute-start.1
  87.6 10.8 %convolution_bitcast_fusion = f32[1,2048,2304]{2,1,0:T(8,128)} fusion(bf16[768,2304]{1,0:T(8,128)(2,1)S(1)} %bitcast.34, bf16[768,2048]{1,0:T(8,128)(2,1)S(1)} %copy-done.5), kind=kOutput, calls=%fused_computation | convolution fusion | flops 7249330176 | bytes 25559040 | tf_op jit(solution)/shard_map/dot_general | solution.py:153
  98.5 19.7 %collective-permute-done.1 = bf16[4,96,1152]{2,1,0:T(8,128)(2,1)S(1)} collective-permute-done((bf16[4,96,1152]{2,1,0:T(8,128)(2,1)S(1)}, bf16[4,96,1152]{2,1,0:T(8,128)(2,1)S(1)}, u32[]{:S(2)}, u32[]{:S(2)}) %collective-permute-start.1) | collective-permute-done | bytes 884768 | tf_op jit(solution)/shard_map/ppermute | solution.py:150
  118.1 1.4 fusion.16
  119.5 0.8 dynamic-slice_bitcast_fusion.3
  120.3 0.0 collective-permute-start.2
  120.3 3.8 %collective-permute-start.4 = (bf16[96,1152]{1,0:T(8,128)(2,1)S(1)}, bf16[96,1152]{1,0:T(8,128)(2,1)S(1)}, u32[]{:S(2)}, u32[]{:S(2)}) collective-permute-start(bf16[96,1152]{1,0:T(8,128)(2,1)S(1)} %get-tuple-element.13), channel_id=1, source_target_pairs={{0,12},{2,14},{4,0},{6,2},{8,4},{10,6},{12,8},{14,10},{1,13},{3,15... | collective-permute-start | bytes 663560 | tf_op jit(solution)/shard_map/ppermute | solution.py:162
  124.1 0.0 collective-permute-start.3
  124.1 10.1 %fusion.17 = f32[1152,2048]{1,0:T(8,128)} fusion(bf16[768,1152]{1,0:T(8,128)(2,1)} %all-gather.2.cloned.1.call-done, bf16[768,2048]{1,0:T(8,128)(2,1)} %copy-done.6), kind=kOutput, calls=%fused_computation.23 | convolution fusion | flops 3623878656 | bytes 14352384 | tf_op jit(solution)/shard_map/dot_general | solution.py:164
  134.2 0.0 collective-permute-done.2
  134.2 0.0 collective-permute-done.4
  134.2 8.3 %collective-permute-done.3 = bf16[96,1152]{1,0:T(8,128)(2,1)} collective-permute-done((bf16[96,1152]{1,0:T(8,128)(2,1)S(1)}, bf16[96,1152]{1,0:T(8,128)(2,1)}, u32[]{:S(2)}, u32[]{:S(2)}) %collective-permute-start.3) | collective-permute-done | bytes 221216 | tf_op jit(solution)/shard_map/ppermute | solution.py:162
  142.5 1.8 %fusion.13 = f32[96,1152]{1,0:T(8,128)} fusion(bf16[96,1152]{1,0:T(8,128)(2,1)S(1)} %collective-permute-done.4, bf16[96,1152]{1,0:T(8,128)(2,1)} %collective-permute-done.3, bf16[96,1152]{1,0:T(8,128)(2,1)S(1)} %collective-permute-done.2, f32[4,96,1152]{2,1,0:T(8,128)S(1)} %get-tuple-element.9, s32[]{:T(128)S(6)} %select_n.39), kind=kLoop, calls=%fused_computation.15 | loop fusion | flops 663552 | bytes 1548292 | tf_op jit(solution)/shard_map/add | solution.py:163
  (10 shorter events, 0.0 us)
Async XLA Ops:
  7.2 48.4 %copy-start = (f32[96,2304]{1,0:T(8,128)S(1)}, f32[96,2304]{1,0:T(8,128)}, u32[]{:S(2)}) copy-start(f32[96,2304]{1,0:T(8,128)} %param.5) | copy-start | bytes 2654212
  7.2 116.9 %all-gather.2.cloned.1.call-start = ((), (), s32[]{:S(2)}) async-start(), calls=%async_computation | async-start | bytes 1990656 | tf_op jit(solution)/shard_map/all_gather | solution.py:132
  7.2 1.2 copy-start.4
  53.7 1.8 %copy-start.2 = (bf16[8,96,2304]{2,1,0:T(8,128)(2,1)}, bf16[8,96,2304]{2,1,0:T(8,128)(2,1)S(1)}, u32[]{:S(2)}) copy-start(bf16[8,96,2304]{2,1,0:T(8,128)(2,1)S(1)} %shard_map.84) | copy-start | bytes 10616836
  68.5 6.0 %collective-permute-start = (bf16[768,2048]{1,0:T(8,128)(2,1)}, bf16[768,2048]{1,0:T(8,128)(2,1)}, u32[]{:S(2)}, u32[]{:S(2)}) collective-permute-start(bf16[768,2048]{1,0:T(8,128)(2,1)} %fusion.7), channel_id=1, source_target_pairs={{0,1},{1,0},{2,3},{3,2},{4,5},{5,4},{6,7},{7,6},{8,9},{9,8},{10,11... | collective-permute-start | bytes 9437192 | tf_op jit(solution)/shard_map/ppermute | solution.py:138
  68.6 12.6 %copy-start.8 = (bf16[2304,2048]{1,0:T(8,128)(2,1)S(1)}, bf16[2304,2048]{1,0:T(8,128)(2,1)}, u32[]{:S(2)}) copy-start(bf16[2304,2048]{1,0:T(8,128)(2,1)} %param.8) | copy-start | bytes 28311556
  81.2 4.3 %copy-start.6 = (bf16[768,2048]{1,0:T(8,128)(2,1)}, bf16[768,2048]{1,0:T(8,128)(2,1)S(1)}, u32[]{:S(2)}) copy-start(bf16[768,2048]{1,0:T(8,128)(2,1)S(1)} %get-tuple-element.11) | copy-start | bytes 9437188
  81.2 6.4 %copy-start.3 = (bf16[8,96,2304]{2,1,0:T(8,128)(2,1)S(1)}, bf16[8,96,2304]{2,1,0:T(8,128)(2,1)}, u32[]{:S(2)}) copy-start(bf16[8,96,2304]{2,1,0:T(8,128)(2,1)} %copy-done.2) | copy-start | bytes 10616836
  81.2 6.4 %copy-start.5 = (bf16[768,2048]{1,0:T(8,128)(2,1)S(1)}, bf16[768,2048]{1,0:T(8,128)(2,1)}, u32[]{:S(2)}) copy-start(bf16[768,2048]{1,0:T(8,128)(2,1)} %param.6) | copy-start | bytes 9437188
  85.5 1.3 copy-start.7
  86.9 31.3 %collective-permute-start.1 = (bf16[4,96,1152]{2,1,0:T(8,128)(2,1)S(1)}, bf16[4,96,1152]{2,1,0:T(8,128)(2,1)S(1)}, u32[]{:S(2)}, u32[]{:S(2)}) collective-permute-start(bf16[4,96,1152]{2,1,0:T(8,128)(2,1)S(1)} %dynamic-slice_bitcast_fusion), channel_id=1, source_target_pairs={{0,2},{2,0},{4,6},{6,4},{8,10},{10,8},{12,14},{14,12},{1,3},{3,1},... | collective-permute-start | bytes 2654216 | tf_op jit(solution)/shard_map/ppermute | solution.py:150
  120.3 14.0 %collective-permute-start.2 = (bf16[96,1152]{1,0:T(8,128)(2,1)}, bf16[96,1152]{1,0:T(8,128)(2,1)S(1)}, u32[]{:S(2)}, u32[]{:S(2)}) collective-permute-start(bf16[96,1152]{1,0:T(8,128)(2,1)} %get-tuple-element.12), channel_id=1, source_target_pairs={{0,4},{2,6},{4,8},{6,10},{8,12},{10,14},{12,0},{14,2},{1,5},{3,7},... | collective-permute-start | bytes 663560 | tf_op jit(solution)/shard_map/ppermute | solution.py:162
  120.3 14.0 %collective-permute-start.4 = (bf16[96,1152]{1,0:T(8,128)(2,1)S(1)}, bf16[96,1152]{1,0:T(8,128)(2,1)S(1)}, u32[]{:S(2)}, u32[]{:S(2)}) collective-permute-start(bf16[96,1152]{1,0:T(8,128)(2,1)S(1)} %get-tuple-element.13), channel_id=1, source_target_pairs={{0,12},{2,14},{4,0},{6,2},{8,4},{10,6},{12,8},{14,10},{1,13},{3,15... | collective-permute-start | bytes 663560 | tf_op jit(solution)/shard_map/ppermute | solution.py:162
  124.1 18.4 %collective-permute-start.3 = (bf16[96,1152]{1,0:T(8,128)(2,1)S(1)}, bf16[96,1152]{1,0:T(8,128)(2,1)}, u32[]{:S(2)}, u32[]{:S(2)}) collective-permute-start(bf16[96,1152]{1,0:T(8,128)(2,1)S(1)} %get-tuple-element.14), channel_id=1, source_target_pairs={{0,8},{2,10},{4,12},{6,14},{8,0},{10,2},{12,4},{14,6},{1,9},{3,11}... | collective-permute-start | bytes 663560 | tf_op jit(solution)/shard_map/ppermute | solution.py:162
  124.1 20.2 %copy-start.1 = (f32[96,2304]{1,0:T(8,128)S(1)}, f32[96,2304]{1,0:T(8,128)}, u32[]{:S(2)}) copy-start(f32[96,2304]{1,0:T(8,128)} %param.5) | copy-start | bytes 2654212
Sparse Core Ops, SparseCore 0:
  68.7 54.7 all-gather.1

commit v2 on v1

--- a/solution.py
+++ b/solution.py
@@ -129,13 +129,19 @@
         jnp.bfloat16
     )
     back_all, input_half = lax.optimization_barrier((back_all, input_half))
-    input_all = lax.all_gather(input_half, "feat", axis=0, tiled=True)
+    line = jnp.zeros((deep, tok, half_width), jnp.bfloat16)
+    line = lax.dynamic_update_index_in_dim(line, input_half, z, 0)
+    for step in range(1, deep):
+        got = lax.ppermute(input_half, "feat", [(i, (i + 2 * step) % n) for i in range(n)])
+        line = lax.dynamic_update_index_in_dim(line, got, lax.rem(z + deep - step, deep), 0)
     back_all = back_all.reshape(n * tok, -1)
 
     partial_value = lax.dot_general(
         back_all, w_dec[0], (((1,), (1,)), ((), ())), preferred_element_type=jnp.float32
     ).astype(jnp.bfloat16)
     other = lax.ppermute(partial_value, "tgt", [(0, 1), (1, 0)])
+    other, line = lax.optimization_barrier((other, line))
+    mates = lax.ppermute(line, "feat", [(i, i ^ 1) for i in range(n)])
     summed = partial_value.astype(jnp.float32) + other.astype(jnp.float32)
     pre_grad = jnp.where(preacts > 0, summed, jnp.zeros_like(summed)).astype(jnp.bfloat16)
     grad_bias = jnp.sum(pre_grad.astype(jnp.float32), axis=0)
@@ -161,6 +167,9 @@
         block = lax.dynamic_index_in_dim(sent, lax.rem(z + step, deep), 0, keepdims=False)
         got = lax.ppermute(block, "feat", [(i, (i + 2 * step) % n) for i in range(n)])
         total = total + got.astype(jnp.float32)
+    input_all = jnp.stack(
+        [jnp.where(y == 0, line, mates), jnp.where(y == 0, mates, line)], axis=1
+    ).reshape(n * tok, half_width)
     grad_enc = lax.dot_general(
         input_all, pre_grad, (((0,), (0,)), ((), ())), preferred_element_type=jnp.float32
     )

time: 151 us -> 148 us (0.980)
  between operations: 14.1 us -> 0.83 us
  waiting for transfers between devices: 33.9 us -> 43.6 us
  starting transfers between devices: 4.61 us -> 9.91 us
  matrix products: 37.5 us -> 33.7 us
  local copies, waits for them, and re-layouts: 5.85 us -> 3.41 us
    ppermute x0 -> x4, waiting for transfers between devices: none -> 18.3 us  [the longest x3 18.3 us: body(): lax.ppermute(input_half, 'feat', [(i, (i + 2 * step) % n) for i in range(...]
    ppermute x1, waiting for transfers between devices: 5.96 us -> 0.01 us  [body(): other = lax.ppermute(partial_value, 'tgt', [(0, 1), (1, 0)])]
    ppermute x1, waiting for transfers between devices: 19.7 us -> 15.8 us  [body(): arrived = lax.ppermute(theirs, 'feat', [(i, i ^ 1) for i in range(n)])]
    dot_general x1, matrix products: 10.1 us -> 6.32 us  [body(): lax.dot_general(input_all, pre_grad, (((0,), (0,)), ((), ())), preferred_...]
    ppermute x0 -> x4, starting transfers between devices: none -> 3.33 us  [the longest x3 2.76 us: body(): lax.ppermute(input_half, 'feat', [(i, (i + 2 * step) % n) for i in range(...]
    another operation x0 -> x2, other arithmetic: none -> 1.7 us  [body(): jnp.stack([jnp.where(y == 0, line, mates), jnp.where(y == 0, mates, line)...]
  transfers between devices with their start and end apart: 6 -> 9, of which waited for: 3 -> 4; matrix products, arithmetic and copies ran while one was open for 23% -> 21% of each run, Pallas kernels for 0% -> 0%
where the time goes in v2:
time: 148 us
  Pallas kernels  45.3 us (31%)
  waiting for transfers between devices  43.6 us (29%)
  matrix products  33.7 us (23%)
  other arithmetic  10.8 us (7%)
  starting transfers between devices  9.91 us (7%)
  local copies, waits for them, and re-layouts  3.41 us (2%)
    pallas_call x1, Pallas kernels, gather(): pl.pallas_call(functools.partial(gather_kernel, n), out_shape=jax.ShapeDt...  45.3 us
    ppermute x3, waiting for transfers between devices, body(): lax.ppermute(input_half, 'feat', [(i, (i + 2 * step) % n) for i in range(...  18.3 us
    ppermute x1, waiting for transfers between devices, body(): arrived = lax.ppermute(theirs, 'feat', [(i, i ^ 1) for i in range(n)])  15.8 us
    dot_general x1, matrix products, body(): lax.dot_general(back_all, w_dec[0], (((1,), (1,)), ((), ())), preferred_e...  12.3 us
    dot_general x1, matrix products, body(): lax.dot_general(active, back_all, (((0,), (0,)), ((), ())), preferred_ele...  10.8 us
    ppermute x3, waiting for transfers between devices, body(): lax.ppermute(block, 'feat', [(i, (i + 2 * step) % n) for i in range(n)])  9.55 us
    reduce_sum x1, other arithmetic, body(): grad_bias = jnp.sum(pre_grad.astype(jnp.float32), axis=0)  6.85 us
    dot_general x1, matrix products, body(): lax.dot_general(input_all, pre_grad, (((0,), (0,)), ((), ())), preferred_...  6.32 us
  transfers between devices with their start and end apart: 9, of which 4 were waited for; matrix products, arithmetic and copies ran while one was open for 21% of the time, Pallas kernels for 0%

profile of v2, /device:TPU:0, one launch (start us, length us, event | category | flops | bytes accessed | tf_op | source)
XLA Modules:
  0.0 147.6 jit_solution(12317033685555218545)
XLA Ops:
  0.6 0.0 copy-start
  0.7 1.2 copy-done.4
  1.9 45.3 %shard_map.84 = bf16[8,96,2304]{2,1,0:T(8,128)(2,1)S(1)} custom-call(f32[96,2304]{1,0:T(8,128)S(1)} %bitcast.50), custom_call_target="tpu_custom_call" | custom-call | bytes 70778880 | tf_op jit(solution)/shard_map/pallas_call | solution.py:97
  47.2 0.0 copy-start.2
  47.2 1.8 %copy-done.2 = bf16[8,96,2304]{2,1,0:T(8,128)(2,1)} copy-done((bf16[8,96,2304]{2,1,0:T(8,128)(2,1)}, bf16[8,96,2304]{2,1,0:T(8,128)(2,1)S(1)}, u32[]{:S(2)}) %copy-start.2) | copy-done | bytes 3538968
  49.0 12.3 %fusion.7 = bf16[768,2048]{1,0:T(8,128)(2,1)} fusion(bf16[768,2304]{1,0:T(8,128)(2,1)} %bitcast.48, bf16[1,2048,2304]{2,1,0:T(8,128)(2,1)} %param.9), kind=kOutput, calls=%fused_computation.8 | convolution fusion | flops 7249330176 | bytes 16121856 | tf_op jit(solution)/shard_map/dot_general | solution.py:139
  61.3 1.7 %collective-permute-start.3 = (bf16[96,1152]{1,0:T(8,128)(2,1)S(1)}, bf16[96,1152]{1,0:T(8,128)(2,1)S(1)}, u32[]{:S(2)}, u32[]{:S(2)}) collective-permute-start(bf16[96,1152]{1,0:T(8,128)(2,1)S(1)} %dynamic-slice_convert_fusion), channel_id=1, source_target_pairs={{0,12},{2,14},{4,0},{6,2},{8,4},{10,6},{12,8},{14,10},{1,13},{3,15... | collective-permute-start | bytes 663560 | tf_op jit(solution)/shard_map/ppermute | solution.py:135
  63.0 1.0 collective-permute-start.1
  64.1 0.1 broadcast_in_dim.23
  64.2 14.7 %collective-permute-done.1 = bf16[96,1152]{1,0:T(8,128)(2,1)S(1)} collective-permute-done((bf16[96,1152]{1,0:T(8,128)(2,1)S(1)}, bf16[96,1152]{1,0:T(8,128)(2,1)S(1)}, u32[]{:S(2)}, u32[]{:S(2)}) %collective-permute-start.1) | collective-permute-done | bytes 221216 | tf_op jit(solution)/shard_map/ppermute | solution.py:135
  78.9 3.6 %collective-permute-done.2 = bf16[96,1152]{1,0:T(8,128)(2,1)S(1)} collective-permute-done((bf16[96,1152]{1,0:T(8,128)(2,1)S(1)}, bf16[96,1152]{1,0:T(8,128)(2,1)S(1)}, u32[]{:S(2)}, u32[]{:S(2)}) %collective-permute-start.2) | collective-permute-done | bytes 221216 | tf_op jit(solution)/shard_map/ppermute | solution.py:135
  82.5 0.0 collective-permute-done.3
  82.6 0.0 copy-start.8
  82.6 0.6 collective-permute-start.4
  83.2 6.9 %convert_reduce_fusion = (f32[2048]{0:T(1024)}, bf16[768,2048]{1,0:T(8,128)(2,1)S(1)}) fusion(bf16[768,2048]{1,0:T(8,128)(2,1)} %collective-permute-done, bf16[768,2048]{1,0:T(8,128)(2,1)} %fusion.7, bf16[768,2048]{1,0:T(8,128)(2,1)} %param.6), kind=kLoop, calls=%fused_computation.3 | loop fusion | flops 12580864 | bytes 12591104 | tf_op jit(solution)/shard_map/reduce_sum | solution.py:147
  90.1 4.3 %fusion.4 = bf16[768,1152]{1,0:T(8,128)(2,1)S(1)} fusion(bf16[768,2048]{1,0:T(8,128)(2,1)S(1)} %get-tuple-element.15, bf16[2304,2048]{1,0:T(8,128)(2,1)S(1)} %copy-done.8, s32[]{:T(128)S(6)} %select_n.51), kind=kOutput, calls=%fused_computation.7 | convolution fusion | flops 3624763392 | bytes 9633796 | tf_op jit(solution)/shard_map/dot_general | solution.py:150
  94.4 0.1 dynamic-slice_bitcast_fusion
  94.4 2.0 %collective-permute-start.5 = (bf16[4,96,1152]{2,1,0:T(8,128)(2,1)S(1)}, bf16[4,96,1152]{2,1,0:T(8,128)(2,1)}, u32[]{:S(2)}, u32[]{:S(2)}) collective-permute-start(bf16[4,96,1152]{2,1,0:T(8,128)(2,1)S(1)} %dynamic-slice_bitcast_fusion), channel_id=1, source_target_pairs={{0,2},{2,0},{4,6},{6,4},{8,10},{10,8},{12,14},{14,12},{1,3},{3,1},... | collective-permute-start | bytes 2654216 | tf_op jit(solution)/shard_map/ppermute | solution.py:156
  96.4 10.8 %convolution_bitcast_fusion = f32[1,2048,2304]{2,1,0:T(8,128)} fusion(bf16[768,2304]{1,0:T(8,128)(2,1)S(1)} %bitcast.49, bf16[768,2048]{1,0:T(8,128)(2,1)S(1)} %copy-done.5), kind=kOutput, calls=%fused_computation | convolution fusion | flops 7249330176 | bytes 25559040 | tf_op jit(solution)/shard_map/dot_general | solution.py:159
  107.2 15.8 %collective-permute-done.5 = bf16[4,96,1152]{2,1,0:T(8,128)(2,1)} collective-permute-done((bf16[4,96,1152]{2,1,0:T(8,128)(2,1)S(1)}, bf16[4,96,1152]{2,1,0:T(8,128)(2,1)}, u32[]{:S(2)}, u32[]{:S(2)}) %collective-permute-start.5) | collective-permute-done | bytes 884768 | tf_op jit(solution)/shard_map/ppermute | solution.py:156
  123.0 1.4 fusion.16
  124.4 0.1 dynamic-slice_bitcast_fusion.3
  124.5 0.7 collective-permute-start.6
  125.2 3.2 %collective-permute-start.8 = (bf16[96,1152]{1,0:T(8,128)(2,1)S(1)}, bf16[96,1152]{1,0:T(8,128)(2,1)S(1)}, u32[]{:S(2)}, u32[]{:S(2)}) collective-permute-start(bf16[96,1152]{1,0:T(8,128)(2,1)S(1)} %get-tuple-element.19), channel_id=1, source_target_pairs={{0,12},{2,14},{4,0},{6,2},{8,4},{10,6},{12,8},{14,10},{1,13},{3,15... | collective-permute-start | bytes 663560 | tf_op jit(solution)/shard_map/ppermute | solution.py:168
  128.4 0.7 collective-permute-start.7
  129.1 0.0 collective-permute-done.4
  129.1 1.5 %select_bitcast_fusion.1 = (bf16[4,1,96,1152]{3,2,1,0:T(8,128)(2,1)S(1)}, bf16[4,1,96,1152]{3,2,1,0:T(8,128)(2,1)S(1)}) fusion(bf16[4,96,1152]{2,1,0:T(8,128)(2,1)S(1)} %bitcast_dynamic-update-slice_fusion, bf16[4,96,1152]{2,1,0:T(8,128)(2,1)} %collective-permute-done.4, pred[]{:T(512)S(6)} %eq.4), kind=kLoop, calls=%fused_computation.15 | loop fusion | flops 884736 | bytes 3538945 | tf_op jit(solution)/shard_map/stack | solution.py:170
  130.6 0.2 pad_maximum_fusion
  130.8 0.0 copy-start.1
  130.8 6.3 %fusion.17 = f32[1152,2048]{1,0:T(8,128)} fusion(bf16[768,1152]{1,0:T(8,128)(2,1)S(1)} %bitcast.51, bf16[768,2048]{1,0:T(8,128)(2,1)S(1)} %copy-done.7), kind=kOutput, calls=%fused_computation.30 | convolution fusion | flops 3623878656 | bytes 14352384 | tf_op jit(solution)/shard_map/dot_general | solution.py:173
  137.2 9.5 %collective-permute-done.7 = bf16[96,1152]{1,0:T(8,128)(2,1)S(1)} collective-permute-done((bf16[96,1152]{1,0:T(8,128)(2,1)S(1)}, bf16[96,1152]{1,0:T(8,128)(2,1)S(1)}, u32[]{:S(2)}, u32[]{:S(2)}) %collective-permute-start.7) | collective-permute-done | bytes 221216 | tf_op jit(solution)/shard_map/ppermute | solution.py:168
  146.7 0.9 fusion.13
  (22 shorter events, 0.2 us)
Async XLA Ops:
  0.6 48.3 %copy-start = (f32[96,2304]{1,0:T(8,128)S(1)}, f32[96,2304]{1,0:T(8,128)}, u32[]{:S(2)}) copy-start(f32[96,2304]{1,0:T(8,128)} %param.5) | copy-start | bytes 2654212
  0.7 1.2 copy-start.4
  47.2 1.8 %copy-start.2 = (bf16[8,96,2304]{2,1,0:T(8,128)(2,1)}, bf16[8,96,2304]{2,1,0:T(8,128)(2,1)S(1)}, u32[]{:S(2)}) copy-start(bf16[8,96,2304]{2,1,0:T(8,128)(2,1)S(1)} %shard_map.84) | copy-start | bytes 10616836
  61.3 21.3 %collective-permute-start = (bf16[768,2048]{1,0:T(8,128)(2,1)}, bf16[768,2048]{1,0:T(8,128)(2,1)}, u32[]{:S(2)}, u32[]{:S(2)}) collective-permute-start(bf16[768,2048]{1,0:T(8,128)(2,1)} %fusion.7), channel_id=1, source_target_pairs={{0,1},{1,0},{2,3},{3,2},{4,5},{5,4},{6,7},{7,6},{8,9},{9,8},{10,11... | collective-permute-start | bytes 9437192 | tf_op jit(solution)/shard_map/ppermute | solution.py:142
  61.3 21.2 %collective-permute-start.3 = (bf16[96,1152]{1,0:T(8,128)(2,1)S(1)}, bf16[96,1152]{1,0:T(8,128)(2,1)S(1)}, u32[]{:S(2)}, u32[]{:S(2)}) collective-permute-start(bf16[96,1152]{1,0:T(8,128)(2,1)S(1)} %dynamic-slice_convert_fusion), channel_id=1, source_target_pairs={{0,12},{2,14},{4,0},{6,2},{8,4},{10,6},{12,8},{14,10},{1,13},{3,15... | collective-permute-start | bytes 663560 | tf_op jit(solution)/shard_map/ppermute | solution.py:135
  63.0 19.5 %collective-permute-start.2 = (bf16[96,1152]{1,0:T(8,128)(2,1)S(1)}, bf16[96,1152]{1,0:T(8,128)(2,1)S(1)}, u32[]{:S(2)}, u32[]{:S(2)}) collective-permute-start(bf16[96,1152]{1,0:T(8,128)(2,1)S(1)} %dynamic-slice_convert_fusion), channel_id=1, source_target_pairs={{0,8},{2,10},{4,12},{6,14},{8,0},{10,2},{12,4},{14,6},{1,9},{3,11}... | collective-permute-start | bytes 663560 | tf_op jit(solution)/shard_map/ppermute | solution.py:135
  63.0 15.9 %collective-permute-start.1 = (bf16[96,1152]{1,0:T(8,128)(2,1)S(1)}, bf16[96,1152]{1,0:T(8,128)(2,1)S(1)}, u32[]{:S(2)}, u32[]{:S(2)}) collective-permute-start(bf16[96,1152]{1,0:T(8,128)(2,1)S(1)} %dynamic-slice_convert_fusion), channel_id=1, source_target_pairs={{0,4},{2,6},{4,8},{6,10},{8,12},{10,14},{12,0},{14,2},{1,5},{3,7},... | collective-permute-start | bytes 663560 | tf_op jit(solution)/shard_map/ppermute | solution.py:135
  82.6 7.5 %copy-start.8 = (bf16[2304,2048]{1,0:T(8,128)(2,1)S(1)}, bf16[2304,2048]{1,0:T(8,128)(2,1)}, u32[]{:S(2)}) copy-start(bf16[2304,2048]{1,0:T(8,128)(2,1)} %param.8) | copy-start | bytes 28311556
  82.6 46.5 %collective-permute-start.4 = (bf16[4,96,1152]{2,1,0:T(8,128)(2,1)S(1)}, bf16[4,96,1152]{2,1,0:T(8,128)(2,1)}, u32[]{:S(2)}, u32[]{:S(2)}) collective-permute-start(bf16[4,96,1152]{2,1,0:T(8,128)(2,1)S(1)} %bitcast_dynamic-update-slice_fusion), channel_id=1, source_target_pairs={{0,2},{2,0},{4,6},{6,4},{8,10},{10,8},{12,14},{14,12},{1,3},{3,1},... | collective-permute-start | bytes 2654216 | tf_op jit(solution)/shard_map/ppermute | solution.py:144
  90.0 4.3 %copy-start.6 = (bf16[768,2048]{1,0:T(8,128)(2,1)}, bf16[768,2048]{1,0:T(8,128)(2,1)S(1)}, u32[]{:S(2)}) copy-start(bf16[768,2048]{1,0:T(8,128)(2,1)S(1)} %get-tuple-element.15) | copy-start | bytes 9437188
  90.0 6.3 %copy-start.3 = (bf16[8,96,2304]{2,1,0:T(8,128)(2,1)S(1)}, bf16[8,96,2304]{2,1,0:T(8,128)(2,1)}, u32[]{:S(2)}) copy-start(bf16[8,96,2304]{2,1,0:T(8,128)(2,1)} %copy-done.2) | copy-start | bytes 10616836
  90.1 6.3 %copy-start.5 = (bf16[768,2048]{1,0:T(8,128)(2,1)S(1)}, bf16[768,2048]{1,0:T(8,128)(2,1)}, u32[]{:S(2)}) copy-start(bf16[768,2048]{1,0:T(8,128)(2,1)} %param.6) | copy-start | bytes 9437188
  94.4 28.6 %collective-permute-start.5 = (bf16[4,96,1152]{2,1,0:T(8,128)(2,1)S(1)}, bf16[4,96,1152]{2,1,0:T(8,128)(2,1)}, u32[]{:S(2)}, u32[]{:S(2)}) collective-permute-start(bf16[4,96,1152]{2,1,0:T(8,128)(2,1)S(1)} %dynamic-slice_bitcast_fusion), channel_id=1, source_target_pairs={{0,2},{2,0},{4,6},{6,4},{8,10},{10,8},{12,14},{14,12},{1,3},{3,1},... | collective-permute-start | bytes 2654216 | tf_op jit(solution)/shard_map/ppermute | solution.py:156
  124.5 12.7 %collective-permute-start.6 = (bf16[96,1152]{1,0:T(8,128)(2,1)S(1)}, bf16[96,1152]{1,0:T(8,128)(2,1)S(1)}, u32[]{:S(2)}, u32[]{:S(2)}) collective-permute-start(bf16[96,1152]{1,0:T(8,128)(2,1)S(1)} %get-tuple-element.18), channel_id=1, source_target_pairs={{0,4},{2,6},{4,8},{6,10},{8,12},{10,14},{12,0},{14,2},{1,5},{3,7},... | collective-permute-start | bytes 663560 | tf_op jit(solution)/shard_map/ppermute | solution.py:168
  125.2 12.0 %collective-permute-start.8 = (bf16[96,1152]{1,0:T(8,128)(2,1)S(1)}, bf16[96,1152]{1,0:T(8,128)(2,1)S(1)}, u32[]{:S(2)}, u32[]{:S(2)}) collective-permute-start(bf16[96,1152]{1,0:T(8,128)(2,1)S(1)} %get-tuple-element.19), channel_id=1, source_target_pairs={{0,12},{2,14},{4,0},{6,2},{8,4},{10,6},{12,8},{14,10},{1,13},{3,15... | collective-permute-start | bytes 663560 | tf_op jit(solution)/shard_map/ppermute | solution.py:168
  128.4 2.5 %copy-start.7 = (bf16[768,2048]{1,0:T(8,128)(2,1)S(1)}, bf16[768,2048]{1,0:T(8,128)(2,1)}, u32[]{:S(2)}) copy-start(bf16[768,2048]{1,0:T(8,128)(2,1)} %copy-done.6) | copy-start | bytes 9437188
  128.4 18.4 %collective-permute-start.7 = (bf16[96,1152]{1,0:T(8,128)(2,1)S(1)}, bf16[96,1152]{1,0:T(8,128)(2,1)S(1)}, u32[]{:S(2)}, u32[]{:S(2)}) collective-permute-start(bf16[96,1152]{1,0:T(8,128)(2,1)S(1)} %get-tuple-element.20), channel_id=1, source_target_pairs={{0,8},{2,10},{4,12},{6,14},{8,0},{10,2},{12,4},{14,6},{1,9},{3,11}... | collective-permute-start | bytes 663560 | tf_op jit(solution)/shard_map/ppermute | solution.py:168
  130.8 16.8 %copy-start.1 = (f32[96,2304]{1,0:T(8,128)S(1)}, f32[96,2304]{1,0:T(8,128)}, u32[]{:S(2)}) copy-start(f32[96,2304]{1,0:T(8,128)} %param.5) | copy-start | bytes 2654212

commit v3 on v1

v3 whole, which is shorter than its diff:
```python
import functools

import jax
import jax.numpy as jnp
from jax import lax
from jax.experimental import pallas as pl
from jax.experimental.pallas import tpu as pltpu
from jax.sharding import PartitionSpec as P

MESH = pl.DeviceIdType.MESH


def gather_kernel(
    n,
    cot_ref, half_ref, dec_ref,
    all_ref, line_ref, part_ref, other_ref,
    dec, dec_sem, up_sem, down_sem, side_sem, recv_sem,
    line_up, line_down, line_recv, swap_send, swap_recv,
):
    deep = n // 2
    tok, width = cot_ref.shape
    f_loc = dec_ref.shape[0]
    tile = min(512, f_loc)
    me = lax.axis_index("feat")
    core = lax.axis_index("tgt")
    z, y = me // 2, lax.rem(me, 2)
    mate = 2 * z + 1 - y
    above, below = z + 1 < deep, z > 0

    def to(block, sem, target):
        return pltpu.make_async_remote_copy(
            src_ref=all_ref.at[block],
            dst_ref=all_ref.at[block],
            send_sem=sem,
            recv_sem=recv_sem.at[block],
            device_id={"feat": target},
            device_id_type=MESH,
        )

    def line_to(row, sem, target):
        return pltpu.make_async_remote_copy(
            src_ref=line_ref.at[row],
            dst_ref=line_ref.at[row],
            send_sem=sem,
            recv_sem=line_recv.at[row],
            device_id={"feat": target},
            device_id_type=MESH,
        )

    def swap(row):
        return pltpu.make_async_remote_copy(
            src_ref=part_ref.at[row],
            dst_ref=other_ref.at[row],
            send_sem=swap_send.at[row],
            recv_sem=swap_recv.at[row],
            device_id={"tgt": 1 - core},
            device_id_type=MESH,
        )

    fetch = pltpu.make_async_copy(dec_ref, dec, dec_sem)
    fetch.start()
    all_ref[me] = cot_ref[...].astype(jnp.bfloat16)
    line_ref[z] = half_ref[...]

    barrier = pltpu.get_barrier_semaphore()
    pl.semaphore_signal(barrier, inc=1, device_id={"feat": mate}, device_id_type=MESH)
    pl.semaphore_signal(barrier, inc=1, device_id={"tgt": 1 - core}, device_id_type=MESH)

    @pl.when(above)
    def _():
        pl.semaphore_signal(barrier, inc=1, device_id={"feat": me + 2}, device_id_type=MESH)

    @pl.when(below)
    def _():
        pl.semaphore_signal(barrier, inc=1, device_id={"feat": me - 2}, device_id_type=MESH)

    pl.semaphore_wait(barrier, 2 + jnp.where(above, 1, 0) + jnp.where(below, 1, 0))

    def place(step):
        away = (step + 1) // 2
        return z + jnp.where(lax.rem(step, 2) == 1, -away, away)

    lag = 3

    @pl.loop(0, 2 * deep - 1 + lag)
    def _(step):
        row = place(step)

        @pl.when((row >= 0) & (row < deep) & (step < 2 * deep - 1))
        def _():
            block = 2 * row + y

            @pl.when(step > 0)
            def _():
                to(block, side_sem.at[row], mate).wait_recv()

            to(block, side_sem.at[row], mate).start()

            @pl.when((row <= z) & above)
            def _():
                to(block, up_sem.at[row], me + 2).start()

            @pl.when((row >= z) & below)
            def _():
                to(block, down_sem.at[row], me - 2).start()

        @pl.when(step == lag)
        def _():
            fetch.wait()

        late = step - lag
        old = place(jnp.maximum(late, 0))

        @pl.when((late >= 0) & (old >= 0) & (old < deep))
        def _():
            @pl.when(late > 0)
            def _():
                line_to(old, line_up.at[old], mate).wait_recv()

            @pl.when((old <= z) & above)
            def _():
                line_to(old, line_up.at[old], me + 2).start()

            @pl.when((old >= z) & below)
            def _():
                line_to(old, line_down.at[old], me - 2).start()

            to(2 * old + 1 - y, side_sem.at[old], mate).wait_recv()
            rows = all_ref[pl.ds(2 * old, 2)].reshape(2 * tok, width)

            @pl.loop(0, f_loc // tile)
            def _(t):
                span = pl.ds(pl.multiple_of(t * tile, tile), tile)
                part_ref[old, :, span] = lax.dot_general(
                    rows, dec[span, :], (((1,), (1,)), ((), ())),
                    preferred_element_type=jnp.float32,
                ).astype(jnp.bfloat16)

            swap(old).start()

    for row in range(deep):
        block = 2 * row + y
        swap(row).wait()
        to(block, side_sem.at[row], mate).wait_send()

        @pl.when((row <= z) & above)
        def _():
            to(block, up_sem.at[row], mate).wait_send()
            line_to(row, line_up.at[row], mate).wait_send()

        @pl.when((row >= z) & below)
        def _():
            to(block, down_sem.at[row], mate).wait_send()
            line_to(row, line_down.at[row], mate).wait_send()


def gather(cot, half, dec, n):
    tok, width = cot.shape
    f_loc = dec.shape[0]
    deep = n // 2
    vmem = pl.BlockSpec(memory_space=pltpu.VMEM)
    chains = [pltpu.SemaphoreType.DMA((deep,))] * 3
    return pl.pallas_call(
        functools.partial(gather_kernel, n),
        out_shape=(
            jax.ShapeDtypeStruct((n, tok, width), jnp.bfloat16),
            jax.ShapeDtypeStruct((deep,) + half.shape, jnp.bfloat16),
            jax.ShapeDtypeStruct((deep, 2 * tok, f_loc), jnp.bfloat16),
            jax.ShapeDtypeStruct((deep, 2 * tok, f_loc), jnp.bfloat16),
        ),
        in_specs=[vmem, vmem, pl.BlockSpec(memory_space=pl.ANY)],
        out_specs=(vmem, vmem, vmem, vmem),
        scratch_shapes=[
            pltpu.VMEM(dec.shape, jnp.bfloat16),
            pltpu.SemaphoreType.DMA,
            *chains,
            pltpu.SemaphoreType.DMA((n,)),
            *chains,
            pltpu.SemaphoreType.DMA((deep,)),
            pltpu.SemaphoreType.DMA((deep,)),
        ],
        compiler_params=pltpu.CompilerParams(
            collective_id=0, has_side_effects=True, vmem_limit_bytes=40 * 1024 * 1024
        ),
        cost_estimate=pl.CostEstimate(
            flops=2 * n * tok * width * f_loc,
            bytes_accessed=40 * n * tok * width,
            transcendentals=0,
        ),
    )(cot, half, dec)


def body(inputs, preacts, cotangent, w_enc, w_dec):
    n = lax.axis_size("feat")
    deep = n // 2
    tok = inputs.shape[0]
    f_loc = preacts.shape[1]
    me = lax.axis_index("feat")
    z, y = me // 2, lax.rem(me, 2)
    tgt_index = lax.axis_index("tgt")
    half_width = inputs.shape[1] // lax.axis_size("tgt")

    input_half = lax.dynamic_slice_in_dim(inputs, tgt_index * half_width, half_width, 1).astype(
        jnp.bfloat16
    )
    back_all, line, partial_value, other = gather(cotangent[0], input_half, w_dec[0], n)
    mates = lax.ppermute(line, "feat", [(i, i ^ 1) for i in range(n)])
    back_all = back_all.reshape(n * tok, -1)
    partial_value = partial_value.reshape(n * tok, f_loc)
    other = other.reshape(n * tok, f_loc)
    summed = partial_value.astype(jnp.float32) + other.astype(jnp.float32)
    pre_grad = jnp.where(preacts > 0, summed, jnp.zeros_like(summed)).astype(jnp.bfloat16)
    grad_bias = jnp.sum(pre_grad.astype(jnp.float32), axis=0)

    enc_half = lax.dynamic_slice_in_dim(w_enc, tgt_index * half_width, half_width, 0)
    part = lax.dot_general(
        pre_grad, enc_half, (((1,), (1,)), ((), ())), preferred_element_type=jnp.float32
    ).astype(jnp.bfloat16)
    part = part.reshape(deep, 2, tok, half_width)
    theirs = lax.dynamic_index_in_dim(part, 1 - y, 1, keepdims=False)
    mine = lax.dynamic_index_in_dim(part, y, 1, keepdims=False)
    arrived = lax.ppermute(theirs, "feat", [(i, i ^ 1) for i in range(n)])

    active = jnp.maximum(preacts, 0)
    grad_dec = lax.dot_general(
        active, back_all, (((0,), (0,)), ((), ())), preferred_element_type=jnp.float32
    )[None]

    both = mine.astype(jnp.float32) + arrived.astype(jnp.float32)
    total = lax.dynamic_index_in_dim(both, z, 0, keepdims=False)
    sent = both.astype(jnp.bfloat16)
    for step in range(1, deep):
        block = lax.dynamic_index_in_dim(sent, lax.rem(z + step, deep), 0, keepdims=False)
        got = lax.ppermute(block, "feat", [(i, (i + 2 * step) % n) for i in range(n)])
        total = total + got.astype(jnp.float32)
    input_all = jnp.stack(
        [jnp.where(y == 0, line, mates), jnp.where(y == 0, mates, line)], axis=1
    ).reshape(n * tok, half_width)
    grad_enc = lax.dot_general(
        input_all, pre_grad, (((0,), (0,)), ((), ())), preferred_element_type=jnp.float32
    )
    return (grad_dec, grad_enc, grad_bias, total)


def solution(mesh):
    in_specs = (
        P(("groups", "feat"), None),
        P("groups", "feat"),
        P("tgt", ("groups", "feat"), None),
        P(None, "feat"),
        P("tgt", "feat", None),
    )
    out_specs = (
        P(("groups", "tgt"), "feat", None),
        P(("groups", "tgt"), "feat"),
        P(("groups", "feat")),
        P(("groups", "feat"), "tgt"),
    )
    return jax.shard_map(body, mesh=mesh, in_specs=in_specs, out_specs=out_specs, check_vma=False)
```

time: 151 us -> 132 us (0.87)
  matrix products: 37.5 us -> 21.4 us
  between operations: 14.1 us -> 0.78 us
  Pallas kernels: 45.3 us -> 57 us
  waiting for transfers between devices: 33.9 us -> 26.1 us
  starting transfers between devices: 4.61 us -> 9.09 us
  local copies, waits for them, and re-layouts: 5.85 us -> 8.82 us
  other arithmetic: 9.83 us -> 8.29 us
    dot_general x1 -> x0, matrix products: 12.3 us -> none  [body(): lax.dot_general(back_all, w_dec[0], (((1,), (1,)), ((), ())), preferred_e...]
    pallas_call x1, Pallas kernels: 45.3 us -> 57 us  [gather(): pl.pallas_call(functools.partial(gather_kernel, n), out_shape=(jax.ShapeD...]
    ppermute x1, waiting for transfers between devices: 19.7 us -> 13.6 us  [body(): arrived = lax.ppermute(theirs, 'feat', [(i, i ^ 1) for i in range(n)])]
    ppermute x1, waiting for transfers between devices: 5.96 us -> 0.01 us  [body(): mates = lax.ppermute(line, 'feat', [(i, i ^ 1) for i in range(n)])]
    reduce_sum x1, other arithmetic: 6.66 us -> 2.09 us  [body(): grad_bias = jnp.sum(pre_grad.astype(jnp.float32), axis=0)]
    ppermute x3, waiting for transfers between devices: 8.27 us -> 12.5 us  [body(): lax.ppermute(block, 'feat', [(i, (i + 2 * step) % n) for i in range(n)])]
    unnamed x18 -> x20, local copies, waits for them, and re-layouts: 4.32 us -> 8.51 us
    dot_general x1, matrix products: 10.1 us -> 6.3 us  [body(): lax.dot_general(input_all, pre_grad, (((0,), (0,)), ((), ())), preferred_...]
  transfers between devices with their start and end apart: 6 -> 5, of which waited for: 3 -> 2; matrix products, arithmetic and copies ran while one was open for 23% -> 22% of each run, Pallas kernels for 0% -> 0%
where the time goes in v3:
time: 132 us
  Pallas kernels  57 us (43%)
  waiting for transfers between devices  26.1 us (20%)
  matrix products  21.4 us (16%)
  starting transfers between devices  9.09 us (7%)
  local copies, waits for them, and re-layouts  8.82 us (7%)
  other arithmetic  8.29 us (6%)
    pallas_call x1, Pallas kernels, gather(): pl.pallas_call(functools.partial(gather_kernel, n), out_shape=(jax.ShapeD...  57 us
    ppermute x1, waiting for transfers between devices, body(): arrived = lax.ppermute(theirs, 'feat', [(i, i ^ 1) for i in range(n)])  13.6 us
    ppermute x3, waiting for transfers between devices, body(): lax.ppermute(block, 'feat', [(i, (i + 2 * step) % n) for i in range(n)])  12.5 us
    dot_general x1, matrix products, body(): lax.dot_general(active, back_all, (((0,), (0,)), ((), ())), preferred_ele...  10.8 us
    unnamed x20, local copies, waits for them, and re-layouts  8.51 us
    ppermute x3, starting transfers between devices, body(): lax.ppermute(block, 'feat', [(i, (i + 2 * step) % n) for i in range(n)])  6.98 us
    dot_general x1, matrix products, body(): lax.dot_general(input_all, pre_grad, (((0,), (0,)), ((), ())), preferred_...  6.3 us
    dot_general x1, matrix products, body(): lax.dot_general(pre_grad, enc_half, (((1,), (1,)), ((), ())), preferred_e...  4.27 us
  transfers between devices with their start and end apart: 5, of which 2 were waited for; matrix products, arithmetic and copies ran while one was open for 22% of the time, Pallas kernels for 0%

profile of v3, /device:TPU:0, one launch (start us, length us, event | category | flops | bytes accessed | tf_op | source)
XLA Modules:
  0.0 131.5 jit_solution(4894876984769982914)
XLA Ops:
  0.6 0.0 copy-start
  0.7 1.2 copy-done
  1.8 0.0 copy-start.3
  1.8 1.2 copy-done.3
  3.0 57.0 %shard_map.84 = (bf16[8,96,2304]{2,1,0:T(8,128)(2,1)S(1)}, bf16[4,96,1152]{2,1,0:T(8,128)(2,1)}, bf16[4,192,2048]{2,1,0:T(8,128)(2,1)S(1)}, bf16[4,192,2048]{2,1,0:T(8,128)(2,1)S(1)}) custom-call(f32[96,2304]{1,0:T(8,128)S(1)} %bitcast.38, bf16[96,1152]{1,0:T(8,128)(2,1)S(1)} %dynamic-slice_convert_fusion.half_ref, bf16[2048,2304]{1,0:T(8,128)(2,1)} %bitcast.43), custom_call_target="tpu_custom_call" | custom-call | flops 7247757312 | bytes 70778880 | tf_op jit(solution)/shard_map/pallas_call | solution.py:163
  60.0 0.0 copy-start.2
  60.1 1.7 %copy-done.2 = bf16[4,192,2048]{2,1,0:T(8,128)(2,1)} copy-done((bf16[4,192,2048]{2,1,0:T(8,128)(2,1)}, bf16[4,192,2048]{2,1,0:T(8,128)(2,1)S(1)}, u32[]{:S(2)}) %copy-start.2) | copy-done | bytes 3145752
  61.7 1.8 %copy-done.4 = bf16[8,96,2304]{2,1,0:T(8,128)(2,1)} copy-done((bf16[8,96,2304]{2,1,0:T(8,128)(2,1)}, bf16[8,96,2304]{2,1,0:T(8,128)(2,1)S(1)}, u32[]{:S(2)}) %copy-start.4) | copy-done | bytes 3538968
  63.5 1.5 %collective-permute-start = (bf16[4,96,1152]{2,1,0:T(8,128)(2,1)}, bf16[4,96,1152]{2,1,0:T(8,128)(2,1)}, u32[]{:S(2)}, u32[]{:S(2)}) collective-permute-start(bf16[4,96,1152]{2,1,0:T(8,128)(2,1)} %get-tuple-element.9), channel_id=1, source_target_pairs={{0,2},{2,0},{4,6},{6,4},{8,10},{10,8},{12,14},{14,12},{1,3},{3,1},... | collective-permute-start | bytes 2654216 | tf_op jit(solution)/shard_map/ppermute | solution.py:207
  65.0 3.3 %convert_add_fusion = bf16[4,192,2048]{2,1,0:T(8,128)(2,1)S(1)} fusion(bf16[4,192,2048]{2,1,0:T(8,128)(2,1)} %copy-done.2, bf16[4,192,2048]{2,1,0:T(8,128)(2,1)S(1)} %get-tuple-element.10), kind=kLoop, calls=%fused_computation.4 | loop fusion | flops 6291456 | bytes 9437184 | tf_op jit(solution)/shard_map/add | solution.py:211
  68.4 0.0 copy-start.9
  68.4 2.1 %convert_reduce_fusion = (f32[2048]{0:T(1024)}, bf16[768,2048]{1,0:T(8,128)(2,1)S(1)}) fusion(bf16[4,192,2048]{2,1,0:T(8,128)(2,1)S(1)} %convert_add_fusion, bf16[768,2048]{1,0:T(8,128)(2,1)S(1)} %copy-done.6), kind=kLoop, calls=%fused_computation.3 | loop fusion | flops 9435136 | bytes 9445376 | tf_op jit(solution)/shard_map/reduce_sum | solution.py:213
  70.5 2.7 %copy-done.9 = bf16[2304,2048]{1,0:T(8,128)(2,1)S(1)} copy-done((bf16[2304,2048]{1,0:T(8,128)(2,1)S(1)}, bf16[2304,2048]{1,0:T(8,128)(2,1)}, u32[]{:S(2)}) %copy-start.9) | copy-done | bytes 9437208
  73.2 4.3 %fusion.3 = bf16[768,1152]{1,0:T(8,128)(2,1)S(1)} fusion(bf16[768,2048]{1,0:T(8,128)(2,1)S(1)} %get-tuple-element.15, bf16[2304,2048]{1,0:T(8,128)(2,1)S(1)} %copy-done.9, s32[]{:T(128)S(6)} %select_n.46), kind=kOutput, calls=%fused_computation.7 | convolution fusion | flops 3624763392 | bytes 9633796 | tf_op jit(solution)/shard_map/dot_general | solution.py:216
  77.5 0.1 dynamic-slice_bitcast_fusion
  77.6 0.6 collective-permute-start.1
  78.2 10.8 %convolution_bitcast_fusion = f32[1,2048,2304]{2,1,0:T(8,128)} fusion(bf16[768,2304]{1,0:T(8,128)(2,1)S(1)} %bitcast.39, bf16[768,2048]{1,0:T(8,128)(2,1)S(1)} %copy-done.6), kind=kOutput, calls=%fused_computation | convolution fusion | flops 7249330176 | bytes 25559040 | tf_op jit(solution)/shard_map/dot_general | solution.py:225
  89.0 0.0 collective-permute-done
  89.0 1.6 %select_bitcast_fusion.1 = (bf16[4,1,96,1152]{3,2,0,1:T(8,128)(2,1)S(1)}, bf16[4,1,96,1152]{3,2,0,1:T(8,128)(2,1)S(1)}) fusion(bf16[4,96,1152]{2,1,0:T(8,128)(2,1)} %get-tuple-element.9, bf16[4,96,1152]{2,1,0:T(8,128)(2,1)} %collective-permute-done, pred[]{:T(512)S(6)} %eq.4), kind=kLoop, calls=%fused_computation.14 | loop fusion | flops 884736 | bytes 3538945 | tf_op jit(solution)/shard_map/stack | solution.py:236
  90.6 0.2 pad_maximum_fusion
  90.8 0.1 copy.9
  91.0 13.6 %collective-permute-done.1 = bf16[4,96,1152]{2,1,0:T(8,128)(2,1)S(1)} collective-permute-done((bf16[4,96,1152]{2,1,0:T(8,128)(2,1)S(1)}, bf16[4,96,1152]{2,1,0:T(8,128)(2,1)S(1)}, u32[]{:S(2)}, u32[]{:S(2)}) %collective-permute-start.1) | collective-permute-done | bytes 884768 | tf_op jit(solution)/shard_map/ppermute | solution.py:222
  104.6 0.2 fusion.12
  104.8 0.1 dynamic-slice_bitcast_fusion.3
  104.9 0.1 collective-permute-start.2
  105.0 6.4 %collective-permute-start.4 = (bf16[96,1152]{1,0:T(8,128)(2,1)S(1)}, bf16[96,1152]{1,0:T(8,128)(2,1)S(1)}, u32[]{:S(2)}, u32[]{:S(2)}) collective-permute-start(bf16[96,1152]{1,0:T(8,128)(2,1)S(1)} %get-tuple-element.19), channel_id=1, source_target_pairs={{0,12},{2,14},{4,0},{6,2},{8,4},{10,6},{12,8},{14,10},{1,13},{3,15... | collective-permute-start | bytes 663560 | tf_op jit(solution)/shard_map/ppermute | solution.py:234
  111.4 0.5 collective-permute-start.3
  111.9 6.3 %fusion.14 = f32[1152,2048]{1,0:T(8,128)} fusion(bf16[768,1152]{1,0:T(8,128)(2,1)S(1)} %bitcast.40, bf16[768,2048]{1,0:T(8,128)(2,1)S(1)} %copy-done.8), kind=kOutput, calls=%fused_computation.25 | convolution fusion | flops 3623878656 | bytes 14352384 | tf_op jit(solution)/shard_map/dot_general | solution.py:239
  118.2 0.0 collective-permute-done.2
  118.2 0.0 collective-permute-done.4
  118.2 12.5 %collective-permute-done.3 = bf16[96,1152]{1,0:T(8,128)(2,1)S(1)} collective-permute-done((bf16[96,1152]{1,0:T(8,128)(2,1)S(1)}, bf16[96,1152]{1,0:T(8,128)(2,1)S(1)}, u32[]{:S(2)}, u32[]{:S(2)}) %collective-permute-start.3) | collective-permute-done | bytes 221216 | tf_op jit(solution)/shard_map/ppermute | solution.py:234
  130.7 0.9 fusion.9
  (12 shorter events, 0.0 us)
Async XLA Ops:
  0.6 1.2 copy-start
  1.8 1.2 copy-start.3
  60.0 1.7 %copy-start.2 = (bf16[4,192,2048]{2,1,0:T(8,128)(2,1)}, bf16[4,192,2048]{2,1,0:T(8,128)(2,1)S(1)}, u32[]{:S(2)}) copy-start(bf16[4,192,2048]{2,1,0:T(8,128)(2,1)S(1)} %get-tuple-element.11) | copy-start | bytes 9437188
  61.7 1.8 %copy-start.4 = (bf16[8,96,2304]{2,1,0:T(8,128)(2,1)}, bf16[8,96,2304]{2,1,0:T(8,128)(2,1)S(1)}, u32[]{:S(2)}) copy-start(bf16[8,96,2304]{2,1,0:T(8,128)(2,1)S(1)} %get-tuple-element.8) | copy-start | bytes 10616836
  63.5 25.5 %collective-permute-start = (bf16[4,96,1152]{2,1,0:T(8,128)(2,1)}, bf16[4,96,1152]{2,1,0:T(8,128)(2,1)}, u32[]{:S(2)}, u32[]{:S(2)}) collective-permute-start(bf16[4,96,1152]{2,1,0:T(8,128)(2,1)} %get-tuple-element.9), channel_id=1, source_target_pairs={{0,2},{2,0},{4,6},{6,4},{8,10},{10,8},{12,14},{14,12},{1,3},{3,1},... | collective-permute-start | bytes 2654216 | tf_op jit(solution)/shard_map/ppermute | solution.py:207
  65.0 3.4 %copy-start.6 = (bf16[768,2048]{1,0:T(8,128)(2,1)S(1)}, bf16[768,2048]{1,0:T(8,128)(2,1)}, u32[]{:S(2)}) copy-start(bf16[768,2048]{1,0:T(8,128)(2,1)} %param.6) | copy-start | bytes 9437188
  68.4 4.8 %copy-start.9 = (bf16[2304,2048]{1,0:T(8,128)(2,1)S(1)}, bf16[2304,2048]{1,0:T(8,128)(2,1)}, u32[]{:S(2)}) copy-start(bf16[2304,2048]{1,0:T(8,128)(2,1)} %param.8) | copy-start | bytes 28311556
  70.5 7.0 %copy-start.7 = (bf16[768,2048]{1,0:T(8,128)(2,1)}, bf16[768,2048]{1,0:T(8,128)(2,1)S(1)}, u32[]{:S(2)}) copy-start(bf16[768,2048]{1,0:T(8,128)(2,1)S(1)} %get-tuple-element.15) | copy-start | bytes 9437188
  73.2 4.9 %copy-start.5 = (bf16[8,96,2304]{2,1,0:T(8,128)(2,1)S(1)}, bf16[8,96,2304]{2,1,0:T(8,128)(2,1)}, u32[]{:S(2)}) copy-start(bf16[8,96,2304]{2,1,0:T(8,128)(2,1)} %copy-done.4) | copy-start | bytes 10616836
  77.6 27.0 %collective-permute-start.1 = (bf16[4,96,1152]{2,1,0:T(8,128)(2,1)S(1)}, bf16[4,96,1152]{2,1,0:T(8,128)(2,1)S(1)}, u32[]{:S(2)}, u32[]{:S(2)}) collective-permute-start(bf16[4,96,1152]{2,1,0:T(8,128)(2,1)S(1)} %dynamic-slice_bitcast_fusion), channel_id=1, source_target_pairs={{0,2},{2,0},{4,6},{6,4},{8,10},{10,8},{12,14},{14,12},{1,3},{3,1},... | collective-permute-start | bytes 2654216 | tf_op jit(solution)/shard_map/ppermute | solution.py:222
  91.0 20.9 %copy-start.8 = (bf16[768,2048]{1,0:T(8,128)(2,1)S(1)}, bf16[768,2048]{1,0:T(8,128)(2,1)}, u32[]{:S(2)}) copy-start(bf16[768,2048]{1,0:T(8,128)(2,1)} %copy-done.7) | copy-start | bytes 9437188
  104.9 13.3 %collective-permute-start.2 = (bf16[96,1152]{1,0:T(8,128)(2,1)S(1)}, bf16[96,1152]{1,0:T(8,128)(2,1)S(1)}, u32[]{:S(2)}, u32[]{:S(2)}) collective-permute-start(bf16[96,1152]{1,0:T(8,128)(2,1)S(1)} %get-tuple-element.18), channel_id=1, source_target_pairs={{0,4},{2,6},{4,8},{6,10},{8,12},{10,14},{12,0},{14,2},{1,5},{3,7},... | collective-permute-start | bytes 663560 | tf_op jit(solution)/shard_map/ppermute | solution.py:234
  105.0 13.2 %collective-permute-start.4 = (bf16[96,1152]{1,0:T(8,128)(2,1)S(1)}, bf16[96,1152]{1,0:T(8,128)(2,1)S(1)}, u32[]{:S(2)}, u32[]{:S(2)}) collective-permute-start(bf16[96,1152]{1,0:T(8,128)(2,1)S(1)} %get-tuple-element.19), channel_id=1, source_target_pairs={{0,12},{2,14},{4,0},{6,2},{8,4},{10,6},{12,8},{14,10},{1,13},{3,15... | collective-permute-start | bytes 663560 | tf_op jit(solution)/shard_map/ppermute | solution.py:234
  111.4 19.3 %collective-permute-start.3 = (bf16[96,1152]{1,0:T(8,128)(2,1)S(1)}, bf16[96,1152]{1,0:T(8,128)(2,1)S(1)}, u32[]{:S(2)}, u32[]{:S(2)}) collective-permute-start(bf16[96,1152]{1,0:T(8,128)(2,1)S(1)} %get-tuple-element.20), channel_id=1, source_target_pairs={{0,8},{2,10},{4,12},{6,14},{8,0},{10,2},{12,4},{14,6},{1,9},{3,11}... | collective-permute-start | bytes 663560 | tf_op jit(solution)/shard_map/ppermute | solution.py:234
  111.9 19.7 %copy-start.1 = (f32[96,2304]{1,0:T(8,128)S(1)}, f32[96,2304]{1,0:T(8,128)}, u32[]{:S(2)}) copy-start(f32[96,2304]{1,0:T(8,128)} %param.5) | copy-start | bytes 2654212

commit v4 on v3

--- a/solution.py
+++ b/solution.py
@@ -217,9 +217,20 @@
         pre_grad, enc_half, (((1,), (1,)), ((), ())), preferred_element_type=jnp.float32
     ).astype(jnp.bfloat16)
     part = part.reshape(deep, 2, tok, half_width)
-    theirs = lax.dynamic_index_in_dim(part, 1 - y, 1, keepdims=False)
-    mine = lax.dynamic_index_in_dim(part, y, 1, keepdims=False)
-    arrived = lax.ppermute(theirs, "feat", [(i, i ^ 1) for i in range(n)])
+    cut = half_width - (half_width * 4 // 9) // 128 * 128
+    across = [(i, i ^ 1) for i in range(n)]
+    along = [[(i, (i + 2 * step) % n) for i in range(n)] for step in range(deep)]
+    first, second = part[..., :cut], part[..., cut:]
+    theirs = lax.dynamic_index_in_dim(first, 1 - y, 1, keepdims=False)
+    mine = lax.dynamic_index_in_dim(first, y, 1, keepdims=False)
+    arrived = lax.ppermute(theirs, "feat", across)
+    pairs = [
+        lax.ppermute(
+            lax.dynamic_index_in_dim(second, lax.rem(z + step, deep), 0, keepdims=False),
+            "feat", along[step],
+        )
+        for step in range(1, deep)
+    ]
 
     active = jnp.maximum(preacts, 0)
     grad_dec = lax.dot_general(
@@ -227,18 +238,33 @@
     )[None]
 
     both = mine.astype(jnp.float32) + arrived.astype(jnp.float32)
-    total = lax.dynamic_index_in_dim(both, z, 0, keepdims=False)
+    pair = lax.dynamic_index_in_dim(second, z, 0, keepdims=False).astype(jnp.float32)
+    for got in pairs:
+        pair = pair + got.astype(jnp.float32)
     sent = both.astype(jnp.bfloat16)
-    for step in range(1, deep):
-        block = lax.dynamic_index_in_dim(sent, lax.rem(z + step, deep), 0, keepdims=False)
-        got = lax.ppermute(block, "feat", [(i, (i + 2 * step) % n) for i in range(n)])
-        total = total + got.astype(jnp.float32)
+    rest = lax.ppermute(
+        lax.dynamic_index_in_dim(pair, 1 - y, 0, keepdims=False).astype(jnp.bfloat16),
+        "feat", across,
+    )
+    blocks = [
+        lax.ppermute(
+            lax.dynamic_index_in_dim(sent, lax.rem(z + step, deep), 0, keepdims=False),
+            "feat", along[step],
+        )
+        for step in range(1, deep)
+    ]
     input_all = jnp.stack(
         [jnp.where(y == 0, line, mates), jnp.where(y == 0, mates, line)], axis=1
     ).reshape(n * tok, half_width)
     grad_enc = lax.dot_general(
         input_all, pre_grad, (((0,), (0,)), ((), ())), preferred_element_type=jnp.float32
     )
+    grad_enc, rest, blocks = lax.optimization_barrier((grad_enc, rest, blocks))
+    total = lax.dynamic_index_in_dim(both, z, 0, keepdims=False)
+    for block in blocks:
+        total = total + block.astype(jnp.float32)
+    rest = lax.dynamic_index_in_dim(pair, y, 0, keepdims=False) + rest.astype(jnp.float32)
+    total = jnp.concatenate([total, rest], axis=1)
     return (grad_dec, grad_enc, grad_bias, total)
 
 

time: 132 us -> 126 us (0.955)
  waiting for transfers between devices: 26.1 us -> 4.61 us
  local copies, waits for them, and re-layouts: 8.82 us -> 17.7 us
  other arithmetic: 8.29 us -> 11 us
  starting transfers between devices: 9.09 us -> 11.6 us
  matrix products: 21.4 us -> 23.2 us
    ppermute x4 -> x8, waiting for transfers between devices: 26.1 us -> 4.6 us  [the longest x3 4.59 us: body(): lax.ppermute(lax.dynamic_index_in_dim(second, lax.rem(z + step, deep), 0,...]
    squeeze x1 -> x2, local copies, waits for them, and re-layouts: 0.08 us -> 3.8 us  [the longest x1 1.94 us: body(): lax.dynamic_index_in_dim(second, lax.rem(z + step, deep), 0, keepdims=False)]
    slice x0 -> x2, local copies, waits for them, and re-layouts: none -> 3.12 us  [body(): first, second = (part[..., :cut], part[..., cut:])]
    ppermute x4 -> x8, starting transfers between devices: 7.54 us -> 10.1 us  [the longest x3 6.93 us: body(): lax.ppermute(lax.dynamic_index_in_dim(second, lax.rem(z + step, deep), 0,...]
    unnamed x20 -> x22, local copies, waits for them, and re-layouts: 8.51 us -> 10.5 us
    dot_general x1, matrix products: 10.8 us -> 12.6 us  [body(): lax.dot_general(active, back_all, (((0,), (0,)), ((), ())), preferred_ele...]
  transfers between devices with their start and end apart: 5 -> 9, of which waited for: 2 -> 1; matrix products, arithmetic and copies ran while one was open for 22% -> 32% of each run, Pallas kernels for 0% -> 0%
where the time goes in v4:
time: 126 us
  Pallas kernels  57 us (45%)
  matrix products  23.2 us (18%)
  local copies, waits for them, and re-layouts  17.7 us (14%)
  starting transfers between devices  11.6 us (9%)
  other arithmetic  11 us (9%)
  waiting for transfers between devices  4.61 us (4%)
    pallas_call x1, Pallas kernels, gather(): pl.pallas_call(functools.partial(gather_kernel, n), out_shape=(jax.ShapeD...  57 us
    dot_general x1, matrix products, body(): lax.dot_general(active, back_all, (((0,), (0,)), ((), ())), preferred_ele...  12.6 us
    unnamed x22, local copies, waits for them, and re-layouts  10.5 us
    ppermute x3, starting transfers between devices, body(): lax.ppermute(lax.dynamic_index_in_dim(second, lax.rem(z + step, deep), 0,...  6.93 us
    dot_general x1, matrix products, body(): lax.dot_general(input_all, pre_grad, (((0,), (0,)), ((), ())), preferred_...  6.3 us
    ppermute x3, waiting for transfers between devices, body(): lax.ppermute(lax.dynamic_index_in_dim(second, lax.rem(z + step, deep), 0,...  4.59 us
    dot_general x1, matrix products, body(): lax.dot_general(pre_grad, enc_half, (((1,), (1,)), ((), ())), preferred_e...  4.29 us
    add x1, other arithmetic, body(): summed = partial_value.astype(jnp.float32) + other.astype(jnp.float32)  3.35 us
  transfers between devices with their start and end apart: 9, of which 1 were waited for; matrix products, arithmetic and copies ran while one was open for 32% of the time, Pallas kernels for 0%

profile of v4, /device:TPU:0, one launch (start us, length us, event | category | flops | bytes accessed | tf_op | source)
XLA Modules:
  0.0 126.0 jit_solution(15352936654010478478)
XLA Ops:
  0.7 1.2 copy-done
  1.8 1.2 copy-done.3
  3.0 57.0 %shard_map.84 = (bf16[8,96,2304]{2,1,0:T(8,128)(2,1)S(1)}, bf16[4,96,1152]{2,1,0:T(8,128)(2,1)}, bf16[4,192,2048]{2,1,0:T(8,128)(2,1)S(1)}, bf16[4,192,2048]{2,1,0:T(8,128)(2,1)S(1)}) custom-call(f32[96,2304]{1,0:T(8,128)S(1)} %bitcast.51, bf16[96,1152]{1,0:T(8,128)(2,1)S(1)} %dynamic-slice_convert_fusion.half_ref, bf16[2048,2304]{1,0:T(8,128)(2,1)} %bitcast.56), custom_call_target="tpu_custom_call" | custom-call | flops 7247757312 | bytes 70778880 | tf_op jit(solution)/shard_map/pallas_call | solution.py:163
  60.0 1.7 %copy-done.2 = bf16[4,192,2048]{2,1,0:T(8,128)(2,1)} copy-done((bf16[4,192,2048]{2,1,0:T(8,128)(2,1)}, bf16[4,192,2048]{2,1,0:T(8,128)(2,1)S(1)}, u32[]{:S(2)}) %copy-start.2) | copy-done | bytes 3145752
  61.7 1.8 %copy-done.4 = bf16[8,96,2304]{2,1,0:T(8,128)(2,1)} copy-done((bf16[8,96,2304]{2,1,0:T(8,128)(2,1)}, bf16[8,96,2304]{2,1,0:T(8,128)(2,1)S(1)}, u32[]{:S(2)}) %copy-start.4) | copy-done | bytes 3538968
  63.5 1.5 %collective-permute-start = (bf16[4,96,1152]{2,1,0:T(8,128)(2,1)}, bf16[4,96,1152]{2,1,0:T(8,128)(2,1)}, u32[]{:S(2)}, u32[]{:S(2)}) collective-permute-start(bf16[4,96,1152]{2,1,0:T(8,128)(2,1)} %get-tuple-element.14), channel_id=1, source_target_pairs={{0,2},{2,0},{4,6},{6,4},{8,10},{10,8},{12,14},{14,12},{1,3},{3,1},... | collective-permute-start | bytes 2654216 | tf_op jit(solution)/shard_map/ppermute | solution.py:207
  65.0 3.3 %convert_add_fusion = bf16[4,192,2048]{2,1,0:T(8,128)(2,1)S(1)} fusion(bf16[4,192,2048]{2,1,0:T(8,128)(2,1)} %copy-done.2, bf16[4,192,2048]{2,1,0:T(8,128)(2,1)S(1)} %get-tuple-element.15), kind=kLoop, calls=%fused_computation.4 | loop fusion | flops 6291456 | bytes 9437184 | tf_op jit(solution)/shard_map/add | solution.py:211
  68.4 2.4 %convert_reduce_fusion = (f32[2048]{0:T(1024)}, bf16[768,2048]{1,0:T(8,128)(2,1)S(1)}) fusion(bf16[4,192,2048]{2,1,0:T(8,128)(2,1)S(1)} %convert_add_fusion, bf16[768,2048]{1,0:T(8,128)(2,1)S(1)} %copy-done.6), kind=kLoop, calls=%fused_computation.3 | loop fusion | flops 9435136 | bytes 9445376 | tf_op jit(solution)/shard_map/reduce_sum | solution.py:213
  70.8 2.0 %copy-done.10 = bf16[2304,2048]{1,0:T(8,128)(2,1)S(1)} copy-done((bf16[2304,2048]{1,0:T(8,128)(2,1)S(1)}, bf16[2304,2048]{1,0:T(8,128)(2,1)}, u32[]{:S(2)}) %copy-start.10) | copy-done | bytes 9437208
  72.8 4.3 %fusion.3 = bf16[768,1152]{1,0:T(8,128)(2,1)S(1)} fusion(bf16[768,2048]{1,0:T(8,128)(2,1)S(1)} %get-tuple-element.23, bf16[2304,2048]{1,0:T(8,128)(2,1)S(1)} %copy-done.10, s32[]{:T(128)S(6)} %select_n.54), kind=kOutput, calls=%fused_computation.7 | convolution fusion | flops 3624763392 | bytes 9633796 | tf_op jit(solution)/shard_map/dot_general | solution.py:216
  77.1 1.2 copy-done.9
  78.3 1.0 slice.9
  79.3 1.9 %dynamic-slice_bitcast_fusion = bf16[4,96,640]{2,1,0:T(8,128)(2,1)} fusion(bf16[4,2,96,640]{3,2,1,0:T(8,128)(2,1)} %slice.9, s32[]{:T(128)S(6)} %select_n.64), kind=kLoop, calls=%fused_computation.14 | loop fusion | bytes 983044 | tf_op jit(solution)/shard_map/jit(dynamic_index_in_dim)/squeeze | solution.py:224
  81.2 0.5 collective-permute-start.5
  81.7 2.1 %slice.8 = bf16[4,2,96,512]{3,2,1,0:T(8,128)(2,1)} slice(bf16[4,2,96,1152]{3,2,1,0:T(8,128)(2,1)} %bitcast.55), slice={[0:4], [0:2], [0:96], [640:1152]} | slice | bytes 1572864 | tf_op jit(solution)/shard_map/slice | solution.py:223
  83.8 1.9 %dynamic-slice_bitcast_fusion.3 = (bf16[2,96,512]{2,1,0:T(8,128)(2,1)}, bf16[2,96,512]{2,1,0:T(8,128)(2,1)}, bf16[2,96,512]{2,1,0:T(8,128)(2,1)}) fusion(bf16[4,2,96,512]{3,2,1,0:T(8,128)(2,1)} %slice.8, s32[]{:T(128)S(6)} %select_n.61, s32[]{:T(128)S(6)} %select_n.63, s32[]{:T(128)S(6)} %select_n.62), kind=kLoop, calls=%fused_computation.27 | loop fusion | bytes 1179660 | tf_op jit(solution)/shard_map/jit(dynamic_index_in_dim)/squeeze | solution.py:229
  85.7 6.4 %collective-permute-start.3 = (bf16[2,96,512]{2,1,0:T(8,128)(2,1)}, bf16[2,96,512]{2,1,0:T(8,128)(2,1)}, u32[]{:S(2)}, u32[]{:S(2)}) collective-permute-start(bf16[2,96,512]{2,1,0:T(8,128)(2,1)} %get-tuple-element.29), channel_id=1, source_target_pairs={{0,12},{2,14},{4,0},{6,2},{8,4},{10,6},{12,8},{14,10},{1,13},{3,15... | collective-permute-start | bytes 589832 | tf_op jit(solution)/shard_map/ppermute | solution.py:228
  92.1 0.6 collective-permute-start.2
  92.6 12.6 %convolution_bitcast_fusion = f32[1,2048,2304]{2,1,0:T(8,128)} fusion(bf16[768,2304]{1,0:T(8,128)(2,1)S(1)} %bitcast.52, bf16[768,2048]{1,0:T(8,128)(2,1)} %param.6), kind=kOutput, calls=%fused_computation | convolution fusion | flops 7249330176 | bytes 25559040 | tf_op jit(solution)/shard_map/dot_general | solution.py:236
  105.3 4.6 %collective-permute-done.2 = bf16[2,96,512]{2,1,0:T(8,128)(2,1)} collective-permute-done((bf16[2,96,512]{2,1,0:T(8,128)(2,1)}, bf16[2,96,512]{2,1,0:T(8,128)(2,1)}, u32[]{:S(2)}, u32[]{:S(2)}) %collective-permute-start.2) | collective-permute-done | bytes 196640 | tf_op jit(solution)/shard_map/ppermute | solution.py:228
  109.9 1.3 %fusion.9 = f32[2,96,512]{2,1,0:T(8,128)S(1)} fusion(bf16[2,96,512]{2,1,0:T(8,128)(2,1)} %collective-permute-done.3, bf16[2,96,512]{2,1,0:T(8,128)(2,1)} %collective-permute-done.2, bf16[2,96,512]{2,1,0:T(8,128)(2,1)} %collective-permute-done.1, bf16[4,2,96,512]{3,2,1,0:T(8,128)(2,1)} %slice.8, s32[]{:T(128)S(6)} %select_n.60), kind=kLoop, calls=%fused_computation.19 | loop fusion | flops 688128 | bytes 1179652 | tf_op jit(solution)/shard_map/add | solution.py:243
  111.2 0.6 collective-permute-start.4
  111.8 1.3 %fusion.16 = (bf16[4,96,640]{2,1,0:T(8,128)(2,1)S(1)}, f32[4,96,640]{2,1,0:T(8,128)S(1)}) fusion(bf16[4,96,640]{2,1,0:T(8,128)(2,1)} %collective-permute-done.5, bf16[4,2,96,640]{3,2,1,0:T(8,128)(2,1)} %slice.9, s32[]{:T(128)S(6)} %select_n.65), kind=kLoop, calls=%fused_computation.34 | loop fusion | flops 983040 | bytes 2457604 | tf_op jit(solution)/shard_map/convert_element_type | solution.py:244
  113.2 0.1 collective-permute-start.7
  113.3 1.9 %collective-permute-start.6 = (bf16[96,640]{1,0:T(8,128)(2,1)S(1)}, bf16[96,640]{1,0:T(8,128)(2,1)S(1)}, u32[]{:S(2)}, u32[]{:S(2)}) collective-permute-start(bf16[96,640]{1,0:T(8,128)(2,1)S(1)} %get-tuple-element.33), channel_id=1, source_target_pairs={{0,4},{2,6},{4,8},{6,10},{8,12},{10,14},{12,0},{14,2},{1,5},{3,7},... | collective-permute-start | bytes 368648 | tf_op jit(solution)/shard_map/ppermute | solution.py:250
  115.2 1.6 %select_bitcast_fusion.1 = (bf16[4,1,96,1152]{3,2,0,1:T(8,128)(2,1)S(1)}, bf16[4,1,96,1152]{3,2,0,1:T(8,128)(2,1)S(1)}) fusion(bf16[4,96,1152]{2,1,0:T(8,128)(2,1)} %get-tuple-element.14, bf16[4,96,1152]{2,1,0:T(8,128)(2,1)} %collective-permute-done, pred[]{:T(512)S(6)} %eq.4), kind=kLoop, calls=%fused_computation.13 | loop fusion | flops 884736 | bytes 3538945 | tf_op jit(solution)/shard_map/stack | solution.py:256
  116.9 0.2 pad_maximum_fusion
  117.0 0.1 copy.9
  117.2 1.5 %copy-done.8 = bf16[768,2048]{1,0:T(8,128)(2,1)S(1)} copy-done((bf16[768,2048]{1,0:T(8,128)(2,1)S(1)}, bf16[768,2048]{1,0:T(8,128)(2,1)}, u32[]{:S(2)}) %copy-start.8) | copy-done | bytes 3145752
  118.7 6.3 %fusion.17 = f32[1152,2048]{1,0:T(8,128)} fusion(bf16[768,1152]{1,0:T(8,128)(2,1)S(1)} %bitcast.53, bf16[768,2048]{1,0:T(8,128)(2,1)S(1)} %copy-done.8), kind=kOutput, calls=%fused_computation.35 | convolution fusion | flops 3623878656 | bytes 14352384 | tf_op jit(solution)/shard_map/dot_general | solution.py:259
  125.1 0.1 fusion.11
  125.2 0.8 pad_maximum_fusion.1
  (29 shorter events, 0.3 us)
Async XLA Ops:
  0.6 1.2 copy-start
  1.8 1.2 copy-start.3
  60.0 1.7 %copy-start.2 = (bf16[4,192,2048]{2,1,0:T(8,128)(2,1)}, bf16[4,192,2048]{2,1,0:T(8,128)(2,1)S(1)}, u32[]{:S(2)}) copy-start(bf16[4,192,2048]{2,1,0:T(8,128)(2,1)S(1)} %get-tuple-element.16) | copy-start | bytes 9437188
  61.7 1.8 %copy-start.4 = (bf16[8,96,2304]{2,1,0:T(8,128)(2,1)}, bf16[8,96,2304]{2,1,0:T(8,128)(2,1)S(1)}, u32[]{:S(2)}) copy-start(bf16[8,96,2304]{2,1,0:T(8,128)(2,1)S(1)} %get-tuple-element.13) | copy-start | bytes 10616836
  63.5 51.8 %collective-permute-start = (bf16[4,96,1152]{2,1,0:T(8,128)(2,1)}, bf16[4,96,1152]{2,1,0:T(8,128)(2,1)}, u32[]{:S(2)}, u32[]{:S(2)}) collective-permute-start(bf16[4,96,1152]{2,1,0:T(8,128)(2,1)} %get-tuple-element.14), channel_id=1, source_target_pairs={{0,2},{2,0},{4,6},{6,4},{8,10},{10,8},{12,14},{14,12},{1,3},{3,1},... | collective-permute-start | bytes 2654216 | tf_op jit(solution)/shard_map/ppermute | solution.py:207
  65.0 3.4 %copy-start.6 = (bf16[768,2048]{1,0:T(8,128)(2,1)S(1)}, bf16[768,2048]{1,0:T(8,128)(2,1)}, u32[]{:S(2)}) copy-start(bf16[768,2048]{1,0:T(8,128)(2,1)} %param.6) | copy-start | bytes 9437188
  68.4 4.4 %copy-start.10 = (bf16[2304,2048]{1,0:T(8,128)(2,1)S(1)}, bf16[2304,2048]{1,0:T(8,128)(2,1)}, u32[]{:S(2)}) copy-start(bf16[2304,2048]{1,0:T(8,128)(2,1)} %param.8) | copy-start | bytes 28311556
  70.8 6.3 %copy-start.7 = (bf16[768,2048]{1,0:T(8,128)(2,1)}, bf16[768,2048]{1,0:T(8,128)(2,1)S(1)}, u32[]{:S(2)}) copy-start(bf16[768,2048]{1,0:T(8,128)(2,1)S(1)} %get-tuple-element.23) | copy-start | bytes 9437188
  77.1 1.2 copy-start.9
  77.1 15.6 %copy-start.5 = (bf16[8,96,2304]{2,1,0:T(8,128)(2,1)S(1)}, bf16[8,96,2304]{2,1,0:T(8,128)(2,1)}, u32[]{:S(2)}) copy-start(bf16[8,96,2304]{2,1,0:T(8,128)(2,1)} %copy-done.4) | copy-start | bytes 10616836
  81.2 30.6 %collective-permute-start.5 = (bf16[4,96,640]{2,1,0:T(8,128)(2,1)}, bf16[4,96,640]{2,1,0:T(8,128)(2,1)}, u32[]{:S(2)}, u32[]{:S(2)}) collective-permute-start(bf16[4,96,640]{2,1,0:T(8,128)(2,1)} %dynamic-slice_bitcast_fusion), channel_id=1, source_target_pairs={{0,2},{2,0},{4,6},{6,4},{8,10},{10,8},{12,14},{14,12},{1,3},{3,1},... | collective-permute-start | bytes 1474568 | tf_op jit(solution)/shard_map/ppermute | solution.py:226
  85.7 19.6 %collective-permute-start.1 = (bf16[2,96,512]{2,1,0:T(8,128)(2,1)}, bf16[2,96,512]{2,1,0:T(8,128)(2,1)}, u32[]{:S(2)}, u32[]{:S(2)}) collective-permute-start(bf16[2,96,512]{2,1,0:T(8,128)(2,1)} %get-tuple-element.28), channel_id=1, source_target_pairs={{0,4},{2,6},{4,8},{6,10},{8,12},{10,14},{12,0},{14,2},{1,5},{3,7},... | collective-permute-start | bytes 589832 | tf_op jit(solution)/shard_map/ppermute | solution.py:228
  85.7 19.6 %collective-permute-start.3 = (bf16[2,96,512]{2,1,0:T(8,128)(2,1)}, bf16[2,96,512]{2,1,0:T(8,128)(2,1)}, u32[]{:S(2)}, u32[]{:S(2)}) collective-permute-start(bf16[2,96,512]{2,1,0:T(8,128)(2,1)} %get-tuple-element.29), channel_id=1, source_target_pairs={{0,12},{2,14},{4,0},{6,2},{8,4},{10,6},{12,8},{14,10},{1,13},{3,15... | collective-permute-start | bytes 589832 | tf_op jit(solution)/shard_map/ppermute | solution.py:228
  92.1 17.8 %collective-permute-start.2 = (bf16[2,96,512]{2,1,0:T(8,128)(2,1)}, bf16[2,96,512]{2,1,0:T(8,128)(2,1)}, u32[]{:S(2)}, u32[]{:S(2)}) collective-permute-start(bf16[2,96,512]{2,1,0:T(8,128)(2,1)} %get-tuple-element.30), channel_id=1, source_target_pairs={{0,8},{2,10},{4,12},{6,14},{8,0},{10,2},{12,4},{14,6},{1,9},{3,11}... | collective-permute-start | bytes 589832 | tf_op jit(solution)/shard_map/ppermute | solution.py:228
  111.2 13.8 %collective-permute-start.4 = (bf16[96,512]{1,0:T(8,128)(2,1)S(1)}, bf16[96,512]{1,0:T(8,128)(2,1)S(1)}, u32[]{:S(2)}, u32[]{:S(2)}) collective-permute-start(bf16[96,512]{1,0:T(8,128)(2,1)S(1)} %fusion.12), channel_id=1, source_target_pairs={{0,2},{2,0},{4,6},{6,4},{8,10},{10,8},{12,14},{14,12},{1,3},{3,1},... | collective-permute-start | bytes 294920 | tf_op jit(solution)/shard_map/ppermute | solution.py:245
  113.2 11.9 %collective-permute-start.8 = (bf16[96,640]{1,0:T(8,128)(2,1)S(1)}, bf16[96,640]{1,0:T(8,128)(2,1)S(1)}, u32[]{:S(2)}, u32[]{:S(2)}) collective-permute-start(bf16[96,640]{1,0:T(8,128)(2,1)S(1)} %get-tuple-element.31), channel_id=1, source_target_pairs={{0,12},{2,14},{4,0},{6,2},{8,4},{10,6},{12,8},{14,10},{1,13},{3,15... | collective-permute-start | bytes 368648 | tf_op jit(solution)/shard_map/ppermute | solution.py:250
  113.2 11.8 %collective-permute-start.7 = (bf16[96,640]{1,0:T(8,128)(2,1)S(1)}, bf16[96,640]{1,0:T(8,128)(2,1)S(1)}, u32[]{:S(2)}, u32[]{:S(2)}) collective-permute-start(bf16[96,640]{1,0:T(8,128)(2,1)S(1)} %get-tuple-element.32), channel_id=1, source_target_pairs={{0,8},{2,10},{4,12},{6,14},{8,0},{10,2},{12,4},{14,6},{1,9},{3,11}... | collective-permute-start | bytes 368648 | tf_op jit(solution)/shard_map/ppermute | solution.py:250
  113.3 11.8 %collective-permute-start.6 = (bf16[96,640]{1,0:T(8,128)(2,1)S(1)}, bf16[96,640]{1,0:T(8,128)(2,1)S(1)}, u32[]{:S(2)}, u32[]{:S(2)}) collective-permute-start(bf16[96,640]{1,0:T(8,128)(2,1)S(1)} %get-tuple-element.33), channel_id=1, source_target_pairs={{0,4},{2,6},{4,8},{6,10},{8,12},{10,14},{12,0},{14,2},{1,5},{3,7},... | collective-permute-start | bytes 368648 | tf_op jit(solution)/shard_map/ppermute | solution.py:250
  116.8 1.9 %copy-start.8 = (bf16[768,2048]{1,0:T(8,128)(2,1)S(1)}, bf16[768,2048]{1,0:T(8,128)(2,1)}, u32[]{:S(2)}) copy-start(bf16[768,2048]{1,0:T(8,128)(2,1)} %copy-done.7) | copy-start | bytes 9437188
  118.7 7.2 %copy-start.1 = (f32[96,2304]{1,0:T(8,128)S(1)}, f32[96,2304]{1,0:T(8,128)}, u32[]{:S(2)}) copy-start(f32[96,2304]{1,0:T(8,128)} %param.5) | copy-start | bytes 2654212

commit v5 on v4

--- a/solution.py
+++ b/solution.py
@@ -212,15 +212,17 @@
     pre_grad = jnp.where(preacts > 0, summed, jnp.zeros_like(summed)).astype(jnp.bfloat16)
     grad_bias = jnp.sum(pre_grad.astype(jnp.float32), axis=0)
 
-    enc_half = lax.dynamic_slice_in_dim(w_enc, tgt_index * half_width, half_width, 0)
-    part = lax.dot_general(
-        pre_grad, enc_half, (((1,), (1,)), ((), ())), preferred_element_type=jnp.float32
-    ).astype(jnp.bfloat16)
-    part = part.reshape(deep, 2, tok, half_width)
     cut = half_width - (half_width * 4 // 9) // 128 * 128
     across = [(i, i ^ 1) for i in range(n)]
     along = [[(i, (i + 2 * step) % n) for i in range(n)] for step in range(deep)]
-    first, second = part[..., :cut], part[..., cut:]
+
+    def columns(start, size):
+        enc_part = lax.dynamic_slice_in_dim(w_enc, tgt_index * half_width + start, size, 0)
+        return lax.dot_general(
+            pre_grad, enc_part, (((1,), (1,)), ((), ())), preferred_element_type=jnp.float32
+        ).astype(jnp.bfloat16).reshape(deep, 2, tok, size)
+
+    first, second = columns(0, cut), columns(cut, half_width - cut)
     theirs = lax.dynamic_index_in_dim(first, 1 - y, 1, keepdims=False)
     mine = lax.dynamic_index_in_dim(first, y, 1, keepdims=False)
     arrived = lax.ppermute(theirs, "feat", across)

time: 126 us -> 125 us (level)
  matrix products: 23.2 us -> 28.8 us
  local copies, waits for them, and re-layouts: 17.7 us -> 12.8 us
  waiting for transfers between devices: 4.61 us -> 0.02 us
  starting transfers between devices: 11.6 us -> 14 us
    dot_general x1 -> x2, matrix products: 4.29 us -> 9.86 us  [columns(): lax.dot_general(pre_grad, enc_part, (((1,), (1,)), ((), ())), preferred_e...]
    ppermute x3, waiting for transfers between devices: 4.59 us -> 0.01 us  [body(): lax.ppermute(lax.dynamic_index_in_dim(second, lax.rem(z + step, deep), 0,...]
    slice x2 -> x0, local copies, waits for them, and re-layouts: 3.12 us -> none  [body(): first, second = (part[..., :cut], part[..., cut:])]
    ppermute x3, starting transfers between devices: 2.07 us -> 4.43 us  [body(): lax.ppermute(lax.dynamic_index_in_dim(sent, lax.rem(z + step, deep), 0, k...]
    unnamed x22 -> x20, local copies, waits for them, and re-layouts: 10.5 us -> 9.85 us
  transfers between devices with their start and end apart: 9 -> 9, of which waited for: 1 -> 0; matrix products, arithmetic and copies ran while one was open for 32% -> 34% of each run, Pallas kernels for 0% -> 0%
where the time goes in v5:
time: 125 us; the launch traced here: 124 us
  Pallas kernels  57 us (46%)
  matrix products  28.8 us (23%)
  starting transfers between devices  14 us (11%)
  local copies, waits for them, and re-layouts  12.8 us (10%)
  other arithmetic  11 us (9%)
    pallas_call x1, Pallas kernels, gather(): pl.pallas_call(functools.partial(gather_kernel, n), out_shape=(jax.ShapeD...  57 us
    dot_general x1, matrix products, body(): lax.dot_general(active, back_all, (((0,), (0,)), ((), ())), preferred_ele...  12.7 us
    dot_general x2, matrix products, columns(): lax.dot_general(pre_grad, enc_part, (((1,), (1,)), ((), ())), preferred_e...  9.86 us
    unnamed x20, local copies, waits for them, and re-layouts  9.85 us
    dot_general x1, matrix products, body(): lax.dot_general(input_all, pre_grad, (((0,), (0,)), ((), ())), preferred_...  6.3 us
    ppermute x3, starting transfers between devices, body(): lax.ppermute(lax.dynamic_index_in_dim(second, lax.rem(z + step, deep), 0,...  5.91 us
    ppermute x3, starting transfers between devices, body(): lax.ppermute(lax.dynamic_index_in_dim(sent, lax.rem(z + step, deep), 0, k...  4.43 us
    add x1, other arithmetic, body(): summed = partial_value.astype(jnp.float32) + other.astype(jnp.float32)  3.35 us
  transfers between devices with their start and end apart: 9, of which 0 were waited for; matrix products, arithmetic and copies ran while one was open for 34% of the time, Pallas kernels for 0%

profile of v5, /device:TPU:0, one launch (start us, length us, event | category | flops | bytes accessed | tf_op | source)
XLA Modules:
  0.0 124.4 jit_solution(16560961507494799605)
XLA Ops:
  0.7 1.2 copy-done
  1.8 1.2 copy-done.3
  3.0 57.0 %shard_map.84 = (bf16[8,96,2304]{2,1,0:T(8,128)(2,1)S(1)}, bf16[4,96,1152]{2,1,0:T(8,128)(2,1)}, bf16[4,192,2048]{2,1,0:T(8,128)(2,1)S(1)}, bf16[4,192,2048]{2,1,0:T(8,128)(2,1)S(1)}) custom-call(f32[96,2304]{1,0:T(8,128)S(1)} %bitcast.53, bf16[96,1152]{1,0:T(8,128)(2,1)S(1)} %dynamic-slice_convert_fusion.half_ref, bf16[2048,2304]{1,0:T(8,128)(2,1)} %bitcast.60), custom_call_target="tpu_custom_call" | custom-call | flops 7247757312 | bytes 70778880 | tf_op jit(solution)/shard_map/pallas_call | solution.py:163
  60.0 1.7 %copy-done.2 = bf16[4,192,2048]{2,1,0:T(8,128)(2,1)} copy-done((bf16[4,192,2048]{2,1,0:T(8,128)(2,1)}, bf16[4,192,2048]{2,1,0:T(8,128)(2,1)S(1)}, u32[]{:S(2)}) %copy-start.2) | copy-done | bytes 3145752
  61.7 1.8 %copy-done.4 = bf16[8,96,2304]{2,1,0:T(8,128)(2,1)} copy-done((bf16[8,96,2304]{2,1,0:T(8,128)(2,1)}, bf16[8,96,2304]{2,1,0:T(8,128)(2,1)S(1)}, u32[]{:S(2)}) %copy-start.4) | copy-done | bytes 3538968
  63.5 1.5 %collective-permute-start = (bf16[4,96,1152]{2,1,0:T(8,128)(2,1)}, bf16[4,96,1152]{2,1,0:T(8,128)(2,1)}, u32[]{:S(2)}, u32[]{:S(2)}) collective-permute-start(bf16[4,96,1152]{2,1,0:T(8,128)(2,1)} %get-tuple-element.14), channel_id=1, source_target_pairs={{0,2},{2,0},{4,6},{6,4},{8,10},{10,8},{12,14},{14,12},{1,3},{3,1},... | collective-permute-start | bytes 2654216 | tf_op jit(solution)/shard_map/ppermute | solution.py:207
  65.0 3.3 %convert_add_fusion = bf16[4,192,2048]{2,1,0:T(8,128)(2,1)S(1)} fusion(bf16[4,192,2048]{2,1,0:T(8,128)(2,1)} %copy-done.2, bf16[4,192,2048]{2,1,0:T(8,128)(2,1)S(1)} %get-tuple-element.15), kind=kLoop, calls=%fused_computation.4 | loop fusion | flops 6291456 | bytes 9437184 | tf_op jit(solution)/shard_map/add | solution.py:211
  68.4 2.4 %convert_reduce_fusion = (f32[2048]{0:T(1024)}, bf16[768,2048]{1,0:T(8,128)(2,1)S(1)}) fusion(bf16[4,192,2048]{2,1,0:T(8,128)(2,1)S(1)} %convert_add_fusion, bf16[768,2048]{1,0:T(8,128)(2,1)S(1)} %copy-done.6), kind=kLoop, calls=%fused_computation.3 | loop fusion | flops 9435136 | bytes 9445376 | tf_op jit(solution)/shard_map/reduce_sum | solution.py:213
  70.7 1.6 %copy-done.7 = bf16[768,2048]{1,0:T(8,128)(2,1)} copy-done((bf16[768,2048]{1,0:T(8,128)(2,1)}, bf16[768,2048]{1,0:T(8,128)(2,1)S(1)}, u32[]{:S(2)}) %copy-start.7) | copy-done | bytes 3145752
  72.4 3.4 %fusion.10 = bf16[768,512]{1,0:T(8,128)(2,1)S(1)} fusion(bf16[768,2048]{1,0:T(8,128)(2,1)S(1)} %get-tuple-element.23, bf16[2304,2048]{1,0:T(8,128)(2,1)} %param.8, s32[]{:T(128)S(6)} %select_n.62), kind=kOutput, calls=%fused_computation.13 | convolution fusion | flops 1611005952 | bytes 6029316 | tf_op jit(solution)/shard_map/dot_general | solution.py:221
  75.8 0.9 copy-done.9
  76.7 0.8 dynamic-slice_bitcast_fusion.3
  77.5 5.3 %collective-permute-start.3 = (bf16[2,96,512]{2,1,0:T(8,128)(2,1)}, bf16[2,96,512]{2,1,0:T(8,128)(2,1)}, u32[]{:S(2)}, u32[]{:S(2)}) collective-permute-start(bf16[2,96,512]{2,1,0:T(8,128)(2,1)} %get-tuple-element.29), channel_id=1, source_target_pairs={{0,12},{2,14},{4,0},{6,2},{8,4},{10,6},{12,8},{14,10},{1,13},{3,15... | collective-permute-start | bytes 589832 | tf_op jit(solution)/shard_map/ppermute | solution.py:230
  82.9 0.6 collective-permute-start.2
  83.4 6.5 %fusion.7 = bf16[768,640]{1,0:T(8,128)(2,1)} fusion(bf16[768,2048]{1,0:T(8,128)(2,1)} %copy-done.7, bf16[2304,2048]{1,0:T(8,128)(2,1)} %param.8, s32[]{:T(128)S(6)} %select_n.57), kind=kOutput, calls=%fused_computation.12 | convolution fusion | flops 2013757440 | bytes 6750212 | tf_op jit(solution)/shard_map/dot_general | solution.py:221
  89.9 1.9 %dynamic-slice_bitcast_fusion = bf16[4,96,640]{2,1,0:T(8,128)(2,1)} fusion(bf16[4,2,96,640]{3,2,1,0:T(8,128)(2,1)} %bitcast.56, s32[]{:T(128)S(6)} %select_n.68), kind=kLoop, calls=%fused_computation.17 | loop fusion | bytes 983044 | tf_op jit(solution)/shard_map/jit(dynamic_index_in_dim)/squeeze | solution.py:226
  91.7 1.5 %collective-permute-start.5 = (bf16[4,96,640]{2,1,0:T(8,128)(2,1)}, bf16[4,96,640]{2,1,0:T(8,128)(2,1)}, u32[]{:S(2)}, u32[]{:S(2)}) collective-permute-start(bf16[4,96,640]{2,1,0:T(8,128)(2,1)} %dynamic-slice_bitcast_fusion), channel_id=1, source_target_pairs={{0,2},{2,0},{4,6},{6,4},{8,10},{10,8},{12,14},{14,12},{1,3},{3,1},... | collective-permute-start | bytes 1474568 | tf_op jit(solution)/shard_map/ppermute | solution.py:228
  93.3 12.7 %convolution_bitcast_fusion = f32[1,2048,2304]{2,1,0:T(8,128)} fusion(bf16[768,2304]{1,0:T(8,128)(2,1)S(1)} %bitcast.54, bf16[768,2048]{1,0:T(8,128)(2,1)} %param.6), kind=kOutput, calls=%fused_computation | convolution fusion | flops 7249330176 | bytes 25559040 | tf_op jit(solution)/shard_map/dot_general | solution.py:238
  105.9 1.3 %fusion.14 = f32[2,96,512]{2,1,0:T(8,128)S(1)} fusion(bf16[2,96,512]{2,1,0:T(8,128)(2,1)} %collective-permute-done.3, bf16[2,96,512]{2,1,0:T(8,128)(2,1)} %collective-permute-done.2, bf16[2,96,512]{2,1,0:T(8,128)(2,1)} %collective-permute-done.1, bf16[4,2,96,512]{3,2,1,0:T(8,128)(2,1)} %bitcast.59, s32[]{:T(128)S(6)} %select_n.64), kind=kLoop, calls=%fused_computation.22 | loop fusion | flops 688128 | bytes 1179652 | tf_op jit(solution)/shard_map/add | solution.py:245
  107.3 0.6 collective-permute-start.4
  107.9 1.3 %fusion.22 = (bf16[4,96,640]{2,1,0:T(8,128)(2,1)S(1)}, f32[4,96,640]{2,1,0:T(8,128)S(1)}) fusion(bf16[4,96,640]{2,1,0:T(8,128)(2,1)} %collective-permute-done.5, bf16[4,2,96,640]{3,2,1,0:T(8,128)(2,1)} %bitcast.57, s32[]{:T(128)S(6)} %select_n.69), kind=kLoop, calls=%fused_computation.38 | loop fusion | flops 983040 | bytes 2457604 | tf_op jit(solution)/shard_map/convert_element_type | solution.py:246
  109.2 0.1 dynamic-slice_bitcast_fusion.4
  109.2 1.5 %collective-permute-start.8 = (bf16[96,640]{1,0:T(8,128)(2,1)S(1)}, bf16[96,640]{1,0:T(8,128)(2,1)S(1)}, u32[]{:S(2)}, u32[]{:S(2)}) collective-permute-start(bf16[96,640]{1,0:T(8,128)(2,1)S(1)} %get-tuple-element.31), channel_id=1, source_target_pairs={{0,12},{2,14},{4,0},{6,2},{8,4},{10,6},{12,8},{14,10},{1,13},{3,15... | collective-permute-start | bytes 368648 | tf_op jit(solution)/shard_map/ppermute | solution.py:252
  110.7 2.0 %collective-permute-start.7 = (bf16[96,640]{1,0:T(8,128)(2,1)S(1)}, bf16[96,640]{1,0:T(8,128)(2,1)S(1)}, u32[]{:S(2)}, u32[]{:S(2)}) collective-permute-start(bf16[96,640]{1,0:T(8,128)(2,1)S(1)} %get-tuple-element.32), channel_id=1, source_target_pairs={{0,8},{2,10},{4,12},{6,14},{8,0},{10,2},{12,4},{14,6},{1,9},{3,11}... | collective-permute-start | bytes 368648 | tf_op jit(solution)/shard_map/ppermute | solution.py:252
  112.8 0.9 collective-permute-start.6
  113.6 1.6 %select_bitcast_fusion.1 = (bf16[4,1,96,1152]{3,2,0,1:T(8,128)(2,1)S(1)}, bf16[4,1,96,1152]{3,2,0,1:T(8,128)(2,1)S(1)}) fusion(bf16[4,96,1152]{2,1,0:T(8,128)(2,1)} %get-tuple-element.14, bf16[4,96,1152]{2,1,0:T(8,128)(2,1)} %collective-permute-done, pred[]{:T(512)S(6)} %eq.4), kind=kLoop, calls=%fused_computation.16 | loop fusion | flops 884736 | bytes 3538945 | tf_op jit(solution)/shard_map/stack | solution.py:258
  115.3 0.2 pad_maximum_fusion
  115.4 0.1 copy.9
  115.6 1.5 %copy-done.8 = bf16[768,2048]{1,0:T(8,128)(2,1)S(1)} copy-done((bf16[768,2048]{1,0:T(8,128)(2,1)S(1)}, bf16[768,2048]{1,0:T(8,128)(2,1)}, u32[]{:S(2)}) %copy-start.8) | copy-done | bytes 3145752
  117.1 6.3 %fusion.23 = f32[1152,2048]{1,0:T(8,128)} fusion(bf16[768,1152]{1,0:T(8,128)(2,1)S(1)} %bitcast.55, bf16[768,2048]{1,0:T(8,128)(2,1)S(1)} %copy-done.8), kind=kOutput, calls=%fused_computation.39 | convolution fusion | flops 3623878656 | bytes 14352384 | tf_op jit(solution)/shard_map/dot_general | solution.py:261
  123.5 0.1 fusion.16
  123.6 0.8 pad_maximum_fusion.1
  (26 shorter events, 0.1 us)
Async XLA Ops:
  0.6 1.2 copy-start
  1.8 1.2 copy-start.3
  60.0 1.7 %copy-start.2 = (bf16[4,192,2048]{2,1,0:T(8,128)(2,1)}, bf16[4,192,2048]{2,1,0:T(8,128)(2,1)S(1)}, u32[]{:S(2)}) copy-start(bf16[4,192,2048]{2,1,0:T(8,128)(2,1)S(1)} %get-tuple-element.16) | copy-start | bytes 9437188
  61.7 1.8 %copy-start.4 = (bf16[8,96,2304]{2,1,0:T(8,128)(2,1)}, bf16[8,96,2304]{2,1,0:T(8,128)(2,1)S(1)}, u32[]{:S(2)}) copy-start(bf16[8,96,2304]{2,1,0:T(8,128)(2,1)S(1)} %get-tuple-element.13) | copy-start | bytes 10616836
  63.5 50.2 %collective-permute-start = (bf16[4,96,1152]{2,1,0:T(8,128)(2,1)}, bf16[4,96,1152]{2,1,0:T(8,128)(2,1)}, u32[]{:S(2)}, u32[]{:S(2)}) collective-permute-start(bf16[4,96,1152]{2,1,0:T(8,128)(2,1)} %get-tuple-element.14), channel_id=1, source_target_pairs={{0,2},{2,0},{4,6},{6,4},{8,10},{10,8},{12,14},{14,12},{1,3},{3,1},... | collective-permute-start | bytes 2654216 | tf_op jit(solution)/shard_map/ppermute | solution.py:207
  65.0 3.4 %copy-start.6 = (bf16[768,2048]{1,0:T(8,128)(2,1)S(1)}, bf16[768,2048]{1,0:T(8,128)(2,1)}, u32[]{:S(2)}) copy-start(bf16[768,2048]{1,0:T(8,128)(2,1)} %param.6) | copy-start | bytes 9437188
  70.7 1.6 %copy-start.7 = (bf16[768,2048]{1,0:T(8,128)(2,1)}, bf16[768,2048]{1,0:T(8,128)(2,1)S(1)}, u32[]{:S(2)}) copy-start(bf16[768,2048]{1,0:T(8,128)(2,1)S(1)} %get-tuple-element.23) | copy-start | bytes 9437188
  75.8 0.9 copy-start.9
  77.5 28.4 %collective-permute-start.1 = (bf16[2,96,512]{2,1,0:T(8,128)(2,1)}, bf16[2,96,512]{2,1,0:T(8,128)(2,1)}, u32[]{:S(2)}, u32[]{:S(2)}) collective-permute-start(bf16[2,96,512]{2,1,0:T(8,128)(2,1)} %get-tuple-element.28), channel_id=1, source_target_pairs={{0,4},{2,6},{4,8},{6,10},{8,12},{10,14},{12,0},{14,2},{1,5},{3,7},... | collective-permute-start | bytes 589832 | tf_op jit(solution)/shard_map/ppermute | solution.py:230
  77.5 28.4 %collective-permute-start.3 = (bf16[2,96,512]{2,1,0:T(8,128)(2,1)}, bf16[2,96,512]{2,1,0:T(8,128)(2,1)}, u32[]{:S(2)}, u32[]{:S(2)}) collective-permute-start(bf16[2,96,512]{2,1,0:T(8,128)(2,1)} %get-tuple-element.29), channel_id=1, source_target_pairs={{0,12},{2,14},{4,0},{6,2},{8,4},{10,6},{12,8},{14,10},{1,13},{3,15... | collective-permute-start | bytes 589832 | tf_op jit(solution)/shard_map/ppermute | solution.py:230
  82.9 23.1 %collective-permute-start.2 = (bf16[2,96,512]{2,1,0:T(8,128)(2,1)}, bf16[2,96,512]{2,1,0:T(8,128)(2,1)}, u32[]{:S(2)}, u32[]{:S(2)}) collective-permute-start(bf16[2,96,512]{2,1,0:T(8,128)(2,1)} %get-tuple-element.30), channel_id=1, source_target_pairs={{0,8},{2,10},{4,12},{6,14},{8,0},{10,2},{12,4},{14,6},{1,9},{3,11}... | collective-permute-start | bytes 589832 | tf_op jit(solution)/shard_map/ppermute | solution.py:230
  83.4 9.8 %copy-start.5 = (bf16[8,96,2304]{2,1,0:T(8,128)(2,1)S(1)}, bf16[8,96,2304]{2,1,0:T(8,128)(2,1)}, u32[]{:S(2)}) copy-start(bf16[8,96,2304]{2,1,0:T(8,128)(2,1)} %copy-done.4) | copy-start | bytes 10616836
  91.7 16.1 %collective-permute-start.5 = (bf16[4,96,640]{2,1,0:T(8,128)(2,1)}, bf16[4,96,640]{2,1,0:T(8,128)(2,1)}, u32[]{:S(2)}, u32[]{:S(2)}) collective-permute-start(bf16[4,96,640]{2,1,0:T(8,128)(2,1)} %dynamic-slice_bitcast_fusion), channel_id=1, source_target_pairs={{0,2},{2,0},{4,6},{6,4},{8,10},{10,8},{12,14},{14,12},{1,3},{3,1},... | collective-permute-start | bytes 1474568 | tf_op jit(solution)/shard_map/ppermute | solution.py:228
  107.3 16.2 %collective-permute-start.4 = (bf16[96,512]{1,0:T(8,128)(2,1)S(1)}, bf16[96,512]{1,0:T(8,128)(2,1)S(1)}, u32[]{:S(2)}, u32[]{:S(2)}) collective-permute-start(bf16[96,512]{1,0:T(8,128)(2,1)S(1)} %fusion.17), channel_id=1, source_target_pairs={{0,2},{2,0},{4,6},{6,4},{8,10},{10,8},{12,14},{14,12},{1,3},{3,1},... | collective-permute-start | bytes 294920 | tf_op jit(solution)/shard_map/ppermute | solution.py:247
  109.2 14.2 %collective-permute-start.8 = (bf16[96,640]{1,0:T(8,128)(2,1)S(1)}, bf16[96,640]{1,0:T(8,128)(2,1)S(1)}, u32[]{:S(2)}, u32[]{:S(2)}) collective-permute-start(bf16[96,640]{1,0:T(8,128)(2,1)S(1)} %get-tuple-element.31), channel_id=1, source_target_pairs={{0,12},{2,14},{4,0},{6,2},{8,4},{10,6},{12,8},{14,10},{1,13},{3,15... | collective-permute-start | bytes 368648 | tf_op jit(solution)/shard_map/ppermute | solution.py:252
  110.7 12.7 %collective-permute-start.7 = (bf16[96,640]{1,0:T(8,128)(2,1)S(1)}, bf16[96,640]{1,0:T(8,128)(2,1)S(1)}, u32[]{:S(2)}, u32[]{:S(2)}) collective-permute-start(bf16[96,640]{1,0:T(8,128)(2,1)S(1)} %get-tuple-element.32), channel_id=1, source_target_pairs={{0,8},{2,10},{4,12},{6,14},{8,0},{10,2},{12,4},{14,6},{1,9},{3,11}... | collective-permute-start | bytes 368648 | tf_op jit(solution)/shard_map/ppermute | solution.py:252
  112.8 10.7 %collective-permute-start.6 = (bf16[96,640]{1,0:T(8,128)(2,1)S(1)}, bf16[96,640]{1,0:T(8,128)(2,1)S(1)}, u32[]{:S(2)}, u32[]{:S(2)}) collective-permute-start(bf16[96,640]{1,0:T(8,128)(2,1)S(1)} %get-tuple-element.33), channel_id=1, source_target_pairs={{0,4},{2,6},{4,8},{6,10},{8,12},{10,14},{12,0},{14,2},{1,5},{3,7},... | collective-permute-start | bytes 368648 | tf_op jit(solution)/shard_map/ppermute | solution.py:252
  115.3 1.9 %copy-start.8 = (bf16[768,2048]{1,0:T(8,128)(2,1)S(1)}, bf16[768,2048]{1,0:T(8,128)(2,1)}, u32[]{:S(2)}) copy-start(bf16[768,2048]{1,0:T(8,128)(2,1)} %copy-done.7) | copy-start | bytes 9437188
  117.1 7.2 %copy-start.1 = (f32[96,2304]{1,0:T(8,128)S(1)}, f32[96,2304]{1,0:T(8,128)}, u32[]{:S(2)}) copy-start(f32[96,2304]{1,0:T(8,128)} %param.5) | copy-start | bytes 2654212
